TPU v7x, 128 devices: a whole 4x4x4 slice. The times are simulated.
128 devices in a mesh: lat: 4 (over x), lon: 32 (over z, y, core).
Axes of the slice: x: 4, y: 4, z: 4, core: 2. Of those that a mesh axis runs over, the one named last changes fastest.
Arguments:
- lattice_feature_values: bfloat16 [131072, 227], P(('lat', 'lon')), may hold values from -6 to 6
- cotangent: bfloat16 [131072, 227], P(('lat', 'lon')), may hold values from -0.0390625 to 0.0390625
- embed_weight: bfloat16 [227, 512], replicated, may hold values from -0.375 to 0.375
- encode_weight: bfloat16 [512, 512], replicated, may hold values from -0.09375 to 0.09375
- sender_weight: bfloat16 [2, 512, 512], replicated, may hold values from -0.25 to 0.25
- receiver_weight: bfloat16 [2, 512, 512], replicated, may hold values from -0.25 to 0.25
- update_weight: bfloat16 [2, 512, 512], replicated, may hold values from -0.09375 to 0.09375
- decode_weight: bfloat16 [512, 227], replicated, may hold values from -0.25 to 0.25
- encode_lists: int32 [512, 64], P(('lat', 'lon')), may hold values from 0 to 1023, as said below
- encode_sources: int32 [32768, 8], P(('lat', 'lon')), may hold values from 0 to 1279, as said below
- mesh_lists: int32 [16384, 4], P(('lat', 'lon')), may hold values from 0 to 255, as said below
- mesh_sources: int32 [32768, 8], P(('lat', 'lon')), may hold values from 0 to 767, as said below
- decode_lists: int32 [512, 64], P(('lat', 'lon')), may hold values from 0 to 255, as said below
- decoder_edge_sources: int32 [131072, 3], P(('lat', 'lon')), may hold values from 0 to 511, as said below
Outputs:
- prediction_field: bfloat16 [131072, 227], P(('lat', 'lon'))
- embed_matrix_slope: float32 [227, 512], P(None, ('lat', 'lon'))
- encode_matrix_slope: float32 [512, 512], P(None, ('lat', 'lon'))
- source_matrix_slope: float32 [2, 512, 512], P(None, None, ('lat', 'lon'))
- target_matrix_slope: float32 [2, 512, 512], P(None, None, ('lat', 'lon'))
- refresh_matrix_slope: float32 [2, 512, 512], P(None, None, ('lat', 'lon'))
- decode_matrix_slope: float32 [512, 227], P(('lat', 'lon'))
Inputs may be any that keep to these rules, and one draw needn't show every extreme that they name: `encode_lists`: row p * 4 + k names rows of device p's own grid points listed for its neighbour in direction k. `encode_sources`: each mesh node has exactly 8 entries, read as in the first step. Every slot that an existing neighbour lists for a device is read by it; no entry names a neighbour beyond the first or last band. `mesh_lists`: row p * 128 + d names rows of device p's own mesh nodes that device d may read. `mesh_sources`: each mesh node has exactly 8 entries. Of the list that device p keeps for device d, d reads a prefix: all 4 slots when p lies beside d in its band or on its sector, or when d lies in one band that the draw chooses, else 1 to 2 slots; every slot of a prefix is read, no slot past it. `decode_lists`: row p * 4 + k names rows of device p's own mesh nodes listed for its neighbour in direction k. `decoder_edge_sources`: each grid point has exactly 3 entries; neighbour slots are read as for encode_sources.
All inputs are finite; a program needn't handle non-finite values.
Results may differ from a plain program's by a relative error of at most 0.015.
Values may be sent and summed in bfloat16 or wider, within the bound.
A program may use at most 128 MiB of HBM per device.

v0:
```python
import jax
import jax.numpy as jnp
from jax import lax
from jax.sharding import PartitionSpec as P


def shifted(value, axis, by):
    length = lax.axis_size(axis)
    return lax.ppermute(value, axis, [(i, (i + by) % length) for i in range(length)])


def shifted_2(block, axis, distance):
    devices = range(lax.axis_size(axis))
    route = [(i - distance, i) for i in devices if i - distance in devices]
    return lax.ppermute(block, axis, route)


def silu_slope(inner):
    sigma = jax.nn.sigmoid(inner)
    return sigma * (1.0 + inner * (1.0 - sigma))


def left_product(first, second):
    return lax.dot_general(
        first, second, (((0,), (0,)), ((), ())), preferred_element_type=jnp.float32
    )


def right_product(first, second):
    return lax.dot_general(
        first, second, (((1,), (1,)), ((), ())), preferred_element_type=jnp.float32
    )


def indicator(indices, width):
    columns = lax.broadcasted_iota(jnp.int32, (indices.shape[0], width), 1)
    return (indices[:, None] == columns).astype(jnp.bfloat16)


def count_matrix(sources, width):
    total = indicator(sources[:, 0], width)
    for column in range(1, sources.shape[1]):
        total = total + indicator(sources[:, column], width)
    return total


def spread_exact(matrix, values):
    high_part = values.astype(jnp.bfloat16)
    low_part = (values - high_part.astype(jnp.float32)).astype(jnp.bfloat16)
    return left_product(matrix, high_part) + left_product(matrix, low_part)


def pass_near(table, lists):
    halo_rows = lists.shape[1]
    columns = table.shape[1]
    payload = table[lists.reshape(-1)].reshape(4, halo_rows, columns)
    cycle_part = [shifted(payload[1 - facing], "lon", 1 - 2 * facing) for facing in (0, 1)]
    band_part = [shifted_2(payload[3 - facing], "lat", 1 - 2 * facing) for facing in (0, 1)]
    return jnp.concatenate(
        [table, cycle_part[0], cycle_part[1], band_part[0], band_part[1]], axis=0
    )


def return_near(grad_ext, lists):
    halo_rows = lists.shape[1]
    columns = grad_ext.shape[1]
    owned = grad_ext.shape[0] - 4 * halo_rows
    blocks = grad_ext[owned:].reshape(4, halo_rows, columns)
    cycle_part = [
        shifted(blocks[facing].astype(jnp.bfloat16), "lon", 2 * facing - 1).astype(jnp.float32)
        for facing in (0, 1)
    ]
    band_part = [
        shifted_2(blocks[2 + facing].astype(jnp.bfloat16), "lat", 2 * facing - 1).astype(
            jnp.float32
        )
        for facing in (0, 1)
    ]
    returned = jnp.concatenate([cycle_part[1], cycle_part[0], band_part[1], band_part[0]], axis=0)
    return grad_ext[:owned] + spread_exact(indicator(lists.reshape(-1), owned), returned)


def pass_rows(table, lists):
    peers, slots = lists.shape
    columns = table.shape[1]
    payload = table[lists.reshape(-1)].reshape(peers, slots, columns)
    arrived = lax.all_to_all(payload, ("lat", "lon"), split_axis=0, concat_axis=0, tiled=True)
    return jnp.concatenate([table, arrived.reshape(peers * slots, columns)], axis=0)


def return_rows(grad_ext, lists):
    peers, slots = lists.shape
    columns = grad_ext.shape[1]
    owned = grad_ext.shape[0] - peers * slots
    outgoing = grad_ext[owned:].reshape(peers, slots, columns)
    returned = lax.all_to_all(
        outgoing.astype(jnp.bfloat16), ("lat", "lon"), split_axis=0, concat_axis=0, tiled=True
    ).astype(outgoing.dtype)
    return grad_ext[:owned] + spread_exact(
        indicator(lists.reshape(-1), owned), returned.reshape(peers * slots, columns)
    )


def on_device(
    lattice_feature_values,
    cotangent,
    embed_weight,
    encode_weight,
    sender_weight,
    receiver_weight,
    update_weight,
    decode_weight,
    encode_lists,
    encode_sources,
    mesh_lists,
    mesh_sources,
    decode_lists,
    decoder_edge_sources,
):
    layers = sender_weight.shape[0]
    degree = mesh_sources.shape[1]
    embed_inner = jnp.dot(lattice_feature_values, embed_weight, preferred_element_type=jnp.float32)
    grid_latent = jax.nn.silu(embed_inner).astype(jnp.bfloat16)
    grid_ext = pass_near(grid_latent, encode_lists)
    encode_counts = count_matrix(encode_sources, grid_ext.shape[0])
    encode_input = jnp.dot(encode_counts, grid_ext, preferred_element_type=jnp.float32).astype(
        jnp.bfloat16
    )
    encode_inner = jnp.dot(encode_input, encode_weight, preferred_element_type=jnp.float32)
    mesh_latent = jax.nn.silu(encode_inner).astype(jnp.bfloat16)
    saved = []
    for layer in range(layers):
        sender_rows = jnp.dot(
            mesh_latent, sender_weight[layer], preferred_element_type=jnp.float32
        ).astype(jnp.bfloat16)
        receiver_rows = jnp.dot(
            mesh_latent, receiver_weight[layer], preferred_element_type=jnp.float32
        )
        sender_ext = pass_rows(sender_rows, mesh_lists)
        fetched = sender_ext[mesh_sources]
        aggregate = jnp.zeros(receiver_rows.shape, jnp.float32)
        for column in range(degree):
            aggregate = aggregate + jax.nn.silu(
                fetched[:, column].astype(jnp.float32) + receiver_rows
            )
        aggregate = aggregate.astype(jnp.bfloat16)
        saved.append((mesh_latent, fetched, sender_ext.shape[0], receiver_rows, aggregate))
        update = jnp.dot(aggregate, update_weight[layer], preferred_element_type=jnp.float32)
        mesh_latent = (mesh_latent.astype(jnp.float32) + update).astype(jnp.bfloat16)
    latent_ext = pass_near(mesh_latent, decode_lists)
    decoder_extended = jnp.dot(
        latent_ext, decode_weight, preferred_element_type=jnp.float32
    ).astype(jnp.bfloat16)
    decode_counts = count_matrix(decoder_edge_sources, decoder_extended.shape[0])
    gathered_sum = jnp.dot(decode_counts, decoder_extended, preferred_element_type=jnp.float32)
    prediction_field = (lattice_feature_values.astype(jnp.float32) + gathered_sum).astype(
        jnp.bfloat16
    )
    decode_back_ext = left_product(decode_counts, cotangent)
    decode_back = return_near(decode_back_ext, decode_lists).astype(jnp.bfloat16)
    decode_matrix_slope = left_product(mesh_latent, decode_back)
    latent_back = right_product(decode_back, decode_weight)
    sender_list, receiver_list, update_list = ([], [], [])
    for layer in reversed(range(layers)):
        old_latent, fetched, ext_rows, receiver_rows, aggregate = saved[layer]
        out_back = latent_back.astype(jnp.bfloat16)
        update_term = left_product(aggregate, out_back)
        aggregate_back = right_product(out_back, update_weight[layer])
        receiver_back = jnp.zeros(receiver_rows.shape, jnp.float32)
        sender_back_ext = jnp.zeros((ext_rows, receiver_rows.shape[1]), jnp.float32)
        for column in range(degree):
            inner = fetched[:, column].astype(jnp.float32) + receiver_rows
            inner_back = aggregate_back * silu_slope(inner)
            receiver_back = receiver_back + inner_back
            sender_back_ext = sender_back_ext + spread_exact(
                indicator(mesh_sources[:, column], ext_rows), inner_back
            )
        sender_b = return_rows(sender_back_ext, mesh_lists).astype(jnp.bfloat16)
        receiver_b = receiver_back.astype(jnp.bfloat16)
        layer_terms = (
            update_term,
            left_product(old_latent, sender_b),
            left_product(old_latent, receiver_b),
        )
        update_list.append(layer_terms[0])
        sender_list.append(layer_terms[1])
        receiver_list.append(layer_terms[2])
        latent_back = latent_back + right_product(sender_b, sender_weight[layer])
        latent_back = latent_back + right_product(receiver_b, receiver_weight[layer])
    encode_back = (latent_back * silu_slope(encode_inner)).astype(jnp.bfloat16)
    encode_matrix_slope = left_product(encode_input, encode_back)
    input_back = right_product(encode_back, encode_weight)
    grid_back_ext = spread_exact(encode_counts, input_back)
    grid_back = return_near(grid_back_ext, encode_lists)
    embed_back = (grid_back * silu_slope(embed_inner)).astype(jnp.bfloat16)
    embed_matrix_slope = left_product(lattice_feature_values, embed_back)
    source_matrix_slope = jnp.stack(sender_list[::-1])
    target_matrix_slope = jnp.stack(receiver_list[::-1])
    refresh_matrix_slope = jnp.stack(update_list[::-1])
    summed_messages = (
        lax.psum_scatter(embed_matrix_slope, ("lat", "lon"), scatter_dimension=1, tiled=True),
        lax.psum_scatter(encode_matrix_slope, ("lat", "lon"), scatter_dimension=1, tiled=True),
        lax.psum_scatter(source_matrix_slope, ("lat", "lon"), scatter_dimension=2, tiled=True),
        lax.psum_scatter(target_matrix_slope, ("lat", "lon"), scatter_dimension=2, tiled=True),
        lax.psum_scatter(refresh_matrix_slope, ("lat", "lon"), scatter_dimension=2, tiled=True),
        lax.psum_scatter(decode_matrix_slope, ("lat", "lon"), scatter_dimension=0, tiled=True),
    )
    return (
        prediction_field,
        summed_messages[0],
        summed_messages[1],
        summed_messages[2],
        summed_messages[3],
        summed_messages[4],
        summed_messages[5],
    )


def solution(mesh):
    return jax.shard_map(
        on_device,
        mesh=mesh,
        in_specs=(
            P(("lat", "lon"), None),
            P(("lat", "lon"), None),
            P(),
            P(),
            P(),
            P(),
            P(),
            P(),
            P(("lat", "lon"), None),
            P(("lat", "lon"), None),
            P(("lat", "lon"), None),
            P(("lat", "lon"), None),
            P(("lat", "lon"), None),
            P(("lat", "lon"), None),
        ),
        out_specs=(
            P(("lat", "lon"), None),
            P(None, ("lat", "lon")),
            P(None, ("lat", "lon")),
            P(None, None, ("lat", "lon")),
            P(None, None, ("lat", "lon")),
            P(None, None, ("lat", "lon")),
            P(("lat", "lon"), None),
        ),
        check_vma=False,
    )
```

profile of v0, /device:TPU:0, one launch (start us, length us, event | category | flops | bytes accessed | tf_op | source)
XLA Modules:
  0.0 394.6 jit_solution(14101413003501161133)
XLA Ops:
  8.0 3.1 constant_dynamic-update-slice_fusion.4
  12.4 6.1 %collective-permute-start.1 = (bf16[64,512]{1,0:T(8,128)(2,1)S(1)}, bf16[64,512]{1,0:T(8,128)(2,1)S(1)}, u32[]{:S(2)}, u32[]{:S(2)}) collective-permute-start(bf16[64,512]{1,0:T(8,128)(2,1)S(1)} %get-tuple-element.81), channel_id=1, source_target_pairs={{0,31},{1,0},{2,1},{3,2},{4,3},{5,4},{6,5},{7,6},{8,7},{9,8},{10,9... | collective-permute-start | bytes 196616 | tf_op jit(solution)/shard_map/ppermute | solution.py:9
  18.5 3.4 collective-permute-start.2
  23.3 2.7 fusion.194
  26.1 4.5 %collective-permute-start.10 = (bf16[64,227]{0,1:T(8,128)(2,1)S(1)}, bf16[64,227]{0,1:T(8,128)(2,1)S(1)}, u32[]{:S(2)}, u32[]{:S(2)}) collective-permute-start(bf16[64,227]{0,1:T(8,128)(2,1)S(1)} %get-tuple-element.85), channel_id=1, source_target_pairs={{0,32},{32,64},{64,96},{1,33},{33,65},{65,97},{2,34},{34,66},{66,9... | collective-permute-start | bytes 87176 | tf_op jit(solution)/shard_map/ppermute | solution.py:15
  33.1 5.1 %collective-permute-start.9 = (bf16[64,227]{0,1:T(8,128)(2,1)S(1)}, bf16[64,227]{0,1:T(8,128)(2,1)S(1)}, u32[]{:S(2)}, u32[]{:S(2)}) collective-permute-start(bf16[64,227]{0,1:T(8,128)(2,1)S(1)} %get-tuple-element.86), channel_id=1, source_target_pairs={{0,31},{1,0},{2,1},{3,2},{4,3},{5,4},{6,5},{7,6},{8,7},{9,8},{10,9... | collective-permute-start | bytes 87176 | tf_op jit(solution)/shard_map/ppermute | solution.py:9
  44.9 6.7 %all-to-all-start = ((bf16[128,4,512]{2,1,0:T(4,128)(2,1)}), bf16[128,4,512]{2,1,0:T(4,128)(2,1)S(1)}, u32[]{:S(2)}, u32[]{:S(2)}) async-start(bf16[128,4,512]{2,1,0:T(4,128)(2,1)} %reshape.209), calls=%async_computation | async-start | bytes 1048576 | tf_op jit(solution)/shard_map/all_to_all | solution.py:87
  54.3 10.8 %all-to-all-done = bf16[128,4,512]{2,1,0:T(4,128)(2,1)S(1)} async-done(((bf16[128,4,512]{2,1,0:T(4,128)(2,1)}), bf16[128,4,512]{2,1,0:T(4,128)(2,1)S(1)}, u32[]{:S(2)}, u32[]{:S(2)}) %all-to-all-start) | async-done | bytes 524320 | tf_op jit(solution)/shard_map/all_to_all | solution.py:87
  65.3 7.5 %gather_fusion.2 = bf16[2048,512]{1,0:T(8,128)(2,1)S(1)} fusion(bf16[768,512]{1,0:T(8,128)(2,1)S(1)} %pad_maximum_fusion.3, s32[2048]{0:T(1024)S(1)} %broadcast_clamp_fusion), kind=kCustom, calls=%fused_computation.2 | custom fusion | bytes 4202496 | tf_op jit(solution)/shard_map/gather | solution.py:140
  72.9 3.8 fusion.186
  83.2 4.9 %all-to-all-start.1 = ((bf16[128,4,512]{2,1,0:T(4,128)(2,1)}), bf16[128,4,512]{2,1,0:T(4,128)(2,1)S(1)}, u32[]{:S(2)}, u32[]{:S(2)}) async-start(bf16[128,4,512]{2,1,0:T(4,128)(2,1)} %reshape.211), calls=%async_computation.1 | async-start | bytes 1048576 | tf_op jit(solution)/shard_map/all_to_all | solution.py:87
  91.6 10.1 %all-to-all-done.1 = bf16[128,4,512]{2,1,0:T(4,128)(2,1)S(1)} async-done(((bf16[128,4,512]{2,1,0:T(4,128)(2,1)}), bf16[128,4,512]{2,1,0:T(4,128)(2,1)S(1)}, u32[]{:S(2)}, u32[]{:S(2)}) %all-to-all-start.1) | async-done | bytes 524320 | tf_op jit(solution)/shard_map/all_to_all | solution.py:87
  101.9 7.5 %gather_fusion.4 = bf16[2048,512]{1,0:T(8,128)(2,1)S(1)} fusion(bf16[768,512]{1,0:T(8,128)(2,1)S(1)} %pad_maximum_fusion.4, s32[2048]{0:T(1024)S(1)} %broadcast_clamp_fusion), kind=kCustom, calls=%fused_computation.4 | custom fusion | bytes 4202496 | tf_op jit(solution)/shard_map/gather | solution.py:140
  109.4 3.8 fusion.185
  113.3 2.8 add_convert_fusion.1
  126.4 6.1 %all-to-all-start.2 = ((bf16[128,4,512]{2,1,0:T(4,128)(2,1)}), bf16[128,4,512]{2,1,0:T(4,128)(2,1)}, u32[]{:S(2)}, u32[]{:S(2)}) async-start(bf16[128,4,512]{2,1,0:T(4,128)(2,1)} %convert_element_type.517), calls=%async_computation.2 | async-start | bytes 1048576 | tf_op jit(solution)/shard_map/all_to_all | solution.py:96
  132.5 2.4 convolution_bitcast_fusion
  138.3 7.3 %all-to-all-done.2 = bf16[128,4,512]{2,1,0:T(4,128)(2,1)} async-done(((bf16[128,4,512]{2,1,0:T(4,128)(2,1)}), bf16[128,4,512]{2,1,0:T(4,128)(2,1)}, u32[]{:S(2)}, u32[]{:S(2)}) %all-to-all-start.2) | async-done | bytes 524320 | tf_op jit(solution)/shard_map/all_to_all | solution.py:96
  151.2 2.5 add_convert_fusion
  163.9 5.7 %all-to-all-start.3 = ((bf16[128,4,512]{2,1,0:T(4,128)(2,1)}), bf16[128,4,512]{2,1,0:T(4,128)(2,1)}, u32[]{:S(2)}, u32[]{:S(2)}) async-start(bf16[128,4,512]{2,1,0:T(4,128)(2,1)} %convert_element_type.546), calls=%async_computation.3 | async-start | bytes 1048576 | tf_op jit(solution)/shard_map/all_to_all | solution.py:96
  171.6 2.5 copy.69
  175.7 2.4 copy.68
  178.2 2.3 convolution_bitcast_fusion.4
  191.8 3.2 fusion.195
  195.8 2.5 copy.67
  198.3 5.1 %collective-permute-start.13 = (bf16[64,512]{1,0:T(8,128)(2,1)}, bf16[64,512]{1,0:T(8,128)(2,1)S(1)}, u32[]{:S(2)}, u32[]{:S(2)}) collective-permute-start(bf16[64,512]{1,0:T(8,128)(2,1)} %get-tuple-element.73), channel_id=1, source_target_pairs={{0,31},{1,0},{2,1},{3,2},{4,3},{5,4},{6,5},{7,6},{8,7},{9,8},{10,9... | collective-permute-start | bytes 196616 | tf_op jit(solution)/shard_map/ppermute | solution.py:9
  203.4 2.5 collective-permute-start.14
  208.0 4.0 %collective-permute-done.15 = bf16[64,512]{1,0:T(8,128)(2,1)S(1)} collective-permute-done((bf16[64,512]{1,0:T(8,128)(2,1)S(1)}, bf16[64,512]{1,0:T(8,128)(2,1)S(1)}, u32[]{:S(2)}, u32[]{:S(2)}) %collective-permute-start.15) | collective-permute-done | bytes 65568 | tf_op jit(solution)/shard_map/ppermute | solution.py:15
  214.6 4.5 %fusion.18 = f32[227,512]{1,0:T(8,128)} fusion(bf16[1024,227]{0,1:T(8,128)(2,1)} %param.14, f32[1280,512]{1,0:T(8,128)S(1)} %copy-done.5, f32[1024,512]{1,0:T(8,128)} %get-tuple-element.108, f32[1024,512]{1,0:T(8,128)} %fusion.28, bf16[256,512]{1,0:T(8,128)(2,1)} %copy-done.39, s32[256]{0:T(256)S(1)} %copy-done.84), kind=kOutput, calls=%fused_computation.59 | convolution fusion | flops 512491520 | bytes 7484416 | tf_op jit(solution)/shard_map/dot_general | solution.py:24
  220.7 5.0 %collective-permute-start.5 = (bf16[64,512]{1,0:T(8,128)(2,1)S(1)}, bf16[64,512]{1,0:T(8,128)(2,1)S(1)}, u32[]{:S(2)}, u32[]{:S(2)}) collective-permute-start(bf16[64,512]{1,0:T(8,128)(2,1)S(1)} %get-tuple-element.77), channel_id=1, source_target_pairs={{0,31},{1,0},{2,1},{3,2},{4,3},{5,4},{6,5},{7,6},{8,7},{9,8},{10,9... | collective-permute-start | bytes 196616 | tf_op jit(solution)/shard_map/ppermute | solution.py:9
  230.3 3.8 collective-permute-done.7
  236.1 143.0 %all-reduce.9.cloned.1.call-done = (f32[227,512]{1,0:T(8,128)}, f32[512,512]{0,1:T(8,128)}, f32[2,512,512]{1,0,2:T(2,128)}, f32[2,512,512]{1,0,2:T(2,128)}, f32[2,512,512]{1,0,2:T(2,128)}, /*index=5*/f32[512,227]{1,0:T(8,128)}) async-done(((f32[227,512]{1,0:T(8,128)}, f32[512,512]{0,1:T(8,128)}, f32[2,512,512]{1,0,2:T(2,128)}, f32[2,512,512]{1,0,2:T(2,128)}, f32[2,512,512]{1,0,2:T(2,128)}, ...) | async-done | bytes 8269840
  (355 shorter events, 90.6 us)
Async XLA Ops:
  7.2 32.9 %copy-start = (bf16[512,512]{1,0:T(8,128)(2,1)S(1)}, bf16[512,512]{1,0:T(8,128)(2,1)}, u32[]{:S(2)}) copy-start(bf16[512,512]{1,0:T(8,128)(2,1)} %param.17) | copy-start | bytes 1572868
  11.1 12.0 %copy-start.64 = (s32[1024,3]{0,1:T(4,128)S(1)}, s32[1024,3]{0,1:T(4,128)}, u32[]{:S(2)}) copy-start(s32[1024,3]{0,1:T(4,128)} %param.27) | copy-start | bytes 36868
  12.3 19.4 %collective-permute-start = (bf16[64,512]{1,0:T(8,128)(2,1)S(1)}, bf16[64,512]{1,0:T(8,128)(2,1)S(1)}, u32[]{:S(2)}, u32[]{:S(2)}) collective-permute-start(bf16[64,512]{1,0:T(8,128)(2,1)S(1)} %get-tuple-element.82), channel_id=1, source_target_pairs={{0,1},{1,2},{2,3},{3,4},{4,5},{5,6},{6,7},{7,8},{8,9},{9,10},{10,1... | collective-permute-start | bytes 196616 | tf_op jit(solution)/shard_map/ppermute | solution.py:9
  12.4 20.6 %collective-permute-start.1 = (bf16[64,512]{1,0:T(8,128)(2,1)S(1)}, bf16[64,512]{1,0:T(8,128)(2,1)S(1)}, u32[]{:S(2)}, u32[]{:S(2)}) collective-permute-start(bf16[64,512]{1,0:T(8,128)(2,1)S(1)} %get-tuple-element.81), channel_id=1, source_target_pairs={{0,31},{1,0},{2,1},{3,2},{4,3},{5,4},{6,5},{7,6},{8,7},{9,8},{10,9... | collective-permute-start | bytes 196616 | tf_op jit(solution)/shard_map/ppermute | solution.py:9
  18.5 14.6 %collective-permute-start.2 = (bf16[64,512]{1,0:T(8,128)(2,1)S(1)}, bf16[64,512]{1,0:T(8,128)(2,1)S(1)}, u32[]{:S(2)}, u32[]{:S(2)}) collective-permute-start(bf16[64,512]{1,0:T(8,128)(2,1)S(1)} %get-tuple-element.80), channel_id=1, source_target_pairs={{0,32},{32,64},{64,96},{1,33},{33,65},{65,97},{2,34},{34,66},{66,9... | collective-permute-start | bytes 196616 | tf_op jit(solution)/shard_map/ppermute | solution.py:15
  21.9 16.4 %collective-permute-start.3 = (bf16[64,512]{1,0:T(8,128)(2,1)S(1)}, bf16[64,512]{1,0:T(8,128)(2,1)S(1)}, u32[]{:S(2)}, u32[]{:S(2)}) collective-permute-start(bf16[64,512]{1,0:T(8,128)(2,1)S(1)} %get-tuple-element.79), channel_id=1, source_target_pairs={{32,0},{64,32},{96,64},{33,1},{65,33},{97,65},{34,2},{66,34},{98,6... | collective-permute-start | bytes 196616 | tf_op jit(solution)/shard_map/ppermute | solution.py:15
  26.1 27.1 %collective-permute-start.10 = (bf16[64,227]{0,1:T(8,128)(2,1)S(1)}, bf16[64,227]{0,1:T(8,128)(2,1)S(1)}, u32[]{:S(2)}, u32[]{:S(2)}) collective-permute-start(bf16[64,227]{0,1:T(8,128)(2,1)S(1)} %get-tuple-element.85), channel_id=1, source_target_pairs={{0,32},{32,64},{64,96},{1,33},{33,65},{65,97},{2,34},{34,66},{66,9... | collective-permute-start | bytes 87176 | tf_op jit(solution)/shard_map/ppermute | solution.py:15
  31.7 21.5 %collective-permute-start.11 = (bf16[64,227]{0,1:T(8,128)(2,1)S(1)}, bf16[64,227]{0,1:T(8,128)(2,1)S(1)}, u32[]{:S(2)}, u32[]{:S(2)}) collective-permute-start(bf16[64,227]{0,1:T(8,128)(2,1)S(1)} %get-tuple-element.84), channel_id=1, source_target_pairs={{32,0},{64,32},{96,64},{33,1},{65,33},{97,65},{34,2},{66,34},{98,6... | collective-permute-start | bytes 87176 | tf_op jit(solution)/shard_map/ppermute | solution.py:15
  33.0 20.2 %collective-permute-start.8 = (bf16[64,227]{0,1:T(8,128)(2,1)S(1)}, bf16[64,227]{0,1:T(8,128)(2,1)S(1)}, u32[]{:S(2)}, u32[]{:S(2)}) collective-permute-start(bf16[64,227]{0,1:T(8,128)(2,1)S(1)} %get-tuple-element.83), channel_id=1, source_target_pairs={{0,1},{1,2},{2,3},{3,4},{4,5},{5,6},{6,7},{7,8},{8,9},{9,10},{10,1... | collective-permute-start | bytes 87176 | tf_op jit(solution)/shard_map/ppermute | solution.py:9
  33.1 20.1 %collective-permute-start.9 = (bf16[64,227]{0,1:T(8,128)(2,1)S(1)}, bf16[64,227]{0,1:T(8,128)(2,1)S(1)}, u32[]{:S(2)}, u32[]{:S(2)}) collective-permute-start(bf16[64,227]{0,1:T(8,128)(2,1)S(1)} %get-tuple-element.86), channel_id=1, source_target_pairs={{0,31},{1,0},{2,1},{3,2},{4,3},{5,4},{6,5},{7,6},{8,7},{9,8},{10,9... | collective-permute-start | bytes 87176 | tf_op jit(solution)/shard_map/ppermute | solution.py:9
  44.9 20.2 %all-to-all-start = ((bf16[128,4,512]{2,1,0:T(4,128)(2,1)}), bf16[128,4,512]{2,1,0:T(4,128)(2,1)S(1)}, u32[]{:S(2)}, u32[]{:S(2)}) async-start(bf16[128,4,512]{2,1,0:T(4,128)(2,1)} %reshape.209), calls=%async_computation | async-start | bytes 1048576 | tf_op jit(solution)/shard_map/all_to_all | solution.py:87
  52.5 12.8 %copy-start.85 = (s32[256]{0:T(256)}, s32[256]{0:T(256)S(1)}, u32[]{:S(2)}) copy-start(s32[256]{0:T(256)S(1)} %eq.289) | copy-start | bytes 3076
  83.2 18.5 %all-to-all-start.1 = ((bf16[128,4,512]{2,1,0:T(4,128)(2,1)}), bf16[128,4,512]{2,1,0:T(4,128)(2,1)S(1)}, u32[]{:S(2)}, u32[]{:S(2)}) async-start(bf16[128,4,512]{2,1,0:T(4,128)(2,1)} %reshape.211), calls=%async_computation.1 | async-start | bytes 1048576 | tf_op jit(solution)/shard_map/all_to_all | solution.py:87
  116.1 18.7 %copy-start.17 = (bf16[256,512]{1,0:T(8,128)(2,1)}, bf16[256,512]{1,0:T(8,128)(2,1)S(1)}, u32[]{:S(2)}) copy-start(bf16[256,512]{1,0:T(8,128)(2,1)S(1)} %get-tuple-element.43) | copy-start | bytes 786436
  126.4 19.2 %all-to-all-start.2 = ((bf16[128,4,512]{2,1,0:T(4,128)(2,1)}), bf16[128,4,512]{2,1,0:T(4,128)(2,1)}, u32[]{:S(2)}, u32[]{:S(2)}) async-start(bf16[128,4,512]{2,1,0:T(4,128)(2,1)} %convert_element_type.517), calls=%async_computation.2 | async-start | bytes 1048576 | tf_op jit(solution)/shard_map/all_to_all | solution.py:96
  163.9 18.9 %all-to-all-start.3 = ((bf16[128,4,512]{2,1,0:T(4,128)(2,1)}), bf16[128,4,512]{2,1,0:T(4,128)(2,1)}, u32[]{:S(2)}, u32[]{:S(2)}) async-start(bf16[128,4,512]{2,1,0:T(4,128)(2,1)} %convert_element_type.546), calls=%async_computation.3 | async-start | bytes 1048576 | tf_op jit(solution)/shard_map/all_to_all | solution.py:96
  169.6 209.4 %all-reduce.9.cloned.1.call-start = ((), (), s32[]{:S(2)}) async-start(), calls=%async_computation.4 | async-start | bytes 16678912
  195.6 11.5 %collective-permute-start.12 = (bf16[64,512]{1,0:T(8,128)(2,1)}, bf16[64,512]{1,0:T(8,128)(2,1)S(1)}, u32[]{:S(2)}, u32[]{:S(2)}) collective-permute-start(bf16[64,512]{1,0:T(8,128)(2,1)} %get-tuple-element.74), channel_id=1, source_target_pairs={{0,1},{1,2},{2,3},{3,4},{4,5},{5,6},{6,7},{7,8},{8,9},{9,10},{10,1... | collective-permute-start | bytes 196616 | tf_op jit(solution)/shard_map/ppermute | solution.py:9
  195.8 16.9 %copy-start.84 = (s32[256]{0:T(256)S(1)}, s32[256]{0:T(256)}, u32[]{:S(2)}) copy-start(s32[256]{0:T(256)} %eq.319) | copy-start | bytes 3076
  198.3 16.3 %copy-start.5 = (f32[1280,512]{1,0:T(8,128)S(1)}, f32[1280,512]{1,0:T(8,128)}, u32[]{:S(2)}) copy-start(f32[1280,512]{1,0:T(8,128)} %get-tuple-element.116) | copy-start | bytes 7864324
  198.3 8.9 %collective-permute-start.13 = (bf16[64,512]{1,0:T(8,128)(2,1)}, bf16[64,512]{1,0:T(8,128)(2,1)S(1)}, u32[]{:S(2)}, u32[]{:S(2)}) collective-permute-start(bf16[64,512]{1,0:T(8,128)(2,1)} %get-tuple-element.73), channel_id=1, source_target_pairs={{0,31},{1,0},{2,1},{3,2},{4,3},{5,4},{6,5},{7,6},{8,7},{9,8},{10,9... | collective-permute-start | bytes 196616 | tf_op jit(solution)/shard_map/ppermute | solution.py:9
  203.4 4.7 %collective-permute-start.14 = (bf16[64,512]{1,0:T(8,128)(2,1)}, bf16[64,512]{1,0:T(8,128)(2,1)S(1)}, u32[]{:S(2)}, u32[]{:S(2)}) collective-permute-start(bf16[64,512]{1,0:T(8,128)(2,1)} %get-tuple-element.72), channel_id=1, source_target_pairs={{0,32},{32,64},{64,96},{1,33},{33,65},{65,97},{2,34},{34,66},{66,9... | collective-permute-start | bytes 196616 | tf_op jit(solution)/shard_map/ppermute | solution.py:15
  205.8 6.2 %collective-permute-start.15 = (bf16[64,512]{1,0:T(8,128)(2,1)S(1)}, bf16[64,512]{1,0:T(8,128)(2,1)S(1)}, u32[]{:S(2)}, u32[]{:S(2)}) collective-permute-start(bf16[64,512]{1,0:T(8,128)(2,1)S(1)} %get-tuple-element.71), channel_id=1, source_target_pairs={{32,0},{64,32},{96,64},{33,1},{65,33},{97,65},{34,2},{66,34},{98,6... | collective-permute-start | bytes 196616 | tf_op jit(solution)/shard_map/ppermute | solution.py:15
  219.1 15.0 %copy-start.47 = (bf16[512,227]{0,1:T(8,128)(2,1)S(1)}, bf16[512,227]{0,1:T(8,128)(2,1)}, u32[]{:S(2)}) copy-start(bf16[512,227]{0,1:T(8,128)(2,1)} %param.21) | copy-start | bytes 697348
  219.1 15.0 %copy-start.88 = (s32[1024,1]{0,1:T(1,128)S(1)}, s32[1024,1]{0,1:T(1,128)}, u32[]{:S(2)}) copy-start(s32[1024,1]{0,1:T(1,128)} %copy-done.87) | copy-start | bytes 12292
  219.1 15.0 %copy-start.90 = (s32[1024,1]{0,1:T(1,128)S(1)}, s32[1024,1]{0,1:T(1,128)}, u32[]{:S(2)}) copy-start(s32[1024,1]{0,1:T(1,128)} %copy-done.89) | copy-start | bytes 12292
  219.1 15.0 %copy-start.92 = (s32[1024,1]{0,1:T(1,128)S(1)}, s32[1024,1]{0,1:T(1,128)}, u32[]{:S(2)}) copy-start(s32[1024,1]{0,1:T(1,128)} %copy-done.91) | copy-start | bytes 12292
  219.1 15.0 %copy-start.99 = (bf16[1024,227]{0,1:T(8,128)(2,1)S(1)}, bf16[1024,227]{0,1:T(8,128)(2,1)}, u32[]{:S(2)}) copy-start(bf16[1024,227]{0,1:T(8,128)(2,1)} %param.14) | copy-start | bytes 1394692
  220.6 8.6 %collective-permute-start.4 = (bf16[64,512]{1,0:T(8,128)(2,1)S(1)}, bf16[64,512]{1,0:T(8,128)(2,1)S(1)}, u32[]{:S(2)}, u32[]{:S(2)}) collective-permute-start(bf16[64,512]{1,0:T(8,128)(2,1)S(1)} %get-tuple-element.78), channel_id=1, source_target_pairs={{0,1},{1,2},{2,3},{3,4},{4,5},{5,6},{6,7},{7,8},{8,9},{9,10},{10,1... | collective-permute-start | bytes 196616 | tf_op jit(solution)/shard_map/ppermute | solution.py:9
  220.7 8.6 %collective-permute-start.5 = (bf16[64,512]{1,0:T(8,128)(2,1)S(1)}, bf16[64,512]{1,0:T(8,128)(2,1)S(1)}, u32[]{:S(2)}, u32[]{:S(2)}) collective-permute-start(bf16[64,512]{1,0:T(8,128)(2,1)S(1)} %get-tuple-element.77), channel_id=1, source_target_pairs={{0,31},{1,0},{2,1},{3,2},{4,3},{5,4},{6,5},{7,6},{8,7},{9,8},{10,9... | collective-permute-start | bytes 196616 | tf_op jit(solution)/shard_map/ppermute | solution.py:9
  225.7 4.5 %collective-permute-start.6 = (bf16[64,512]{1,0:T(8,128)(2,1)S(1)}, bf16[64,512]{1,0:T(8,128)(2,1)S(1)}, u32[]{:S(2)}, u32[]{:S(2)}) collective-permute-start(bf16[64,512]{1,0:T(8,128)(2,1)S(1)} %get-tuple-element.76), channel_id=1, source_target_pairs={{0,32},{32,64},{64,96},{1,33},{33,65},{65,97},{2,34},{34,66},{66,9... | collective-permute-start | bytes 196616 | tf_op jit(solution)/shard_map/ppermute | solution.py:15
  227.9 6.2 %collective-permute-start.7 = (bf16[64,512]{1,0:T(8,128)(2,1)S(1)}, bf16[64,512]{1,0:T(8,128)(2,1)S(1)}, u32[]{:S(2)}, u32[]{:S(2)}) collective-permute-start(bf16[64,512]{1,0:T(8,128)(2,1)S(1)} %get-tuple-element.75), channel_id=1, source_target_pairs={{32,0},{64,32},{96,64},{33,1},{65,33},{97,65},{34,2},{66,34},{98,6... | collective-permute-start | bytes 196616 | tf_op jit(solution)/shard_map/ppermute | solution.py:15
  (91 other events, 336.4 us)
Sparse Core Ops, SparseCore 0:
  219.2 159.8 all-reduce.8
where the time goes:
time: 402 us; the launch traced here: 395 us
  waiting for transfers between devices  183 us (46%)
  matrix products  68.6 us (17%)
  starting transfers between devices  63 us (16%)
  local copies, waits for them, and re-layouts  60.9 us (15%)
  between operations  16.3 us (4%)
    unnamed x2, waiting for transfers between devices  143 us
    dot_general x51, matrix products, left_product(): lax.dot_general(first, second, (((0,), (0,)), ((), ())), preferred_elemen...  47.6 us
    ppermute x8, starting transfers between devices, shifted(): lax.ppermute(value, axis, [(i, (i + by) % length) for i in range(length)])  21.5 us
    all_to_all x2, waiting for transfers between devices, pass_rows(): lax.all_to_all(payload, ('lat', 'lon'), split_axis=0, concat_axis=0, tile...  20.9 us
    ppermute x8, starting transfers between devices, shifted_2(): return lax.ppermute(block, axis, route)  17.7 us
    gather x2, local copies, waits for them, and re-layouts, on_device(): fetched = sender_ext[mesh_sources]  15.1 us
    unnamed x224, local copies, waits for them, and re-layouts  14 us
    all_to_all x2, starting transfers between devices, return_rows(): lax.all_to_all(outgoing.astype(jnp.bfloat16), ('lat', 'lon'), split_axis=...  11.8 us
  transfers between devices with their start and end apart: 21, of which 9 were waited for; matrix products, arithmetic and copies ran while one was open for 10% of the time, Pallas kernels for 0%

commit v1 on v0

v1 whole, which is shorter than its diff:
```python
import functools

import jax
import jax.numpy as jnp
from jax import lax
from jax.experimental import pallas as pl
from jax.experimental.pallas import tpu as pltpu
from jax.sharding import PartitionSpec as P

BF = jnp.bfloat16
F32 = jnp.float32
MESH = pl.DeviceIdType.MESH

BANDS, SECTORS, PEERS = 4, 32, 128
LATENT, CHANNELS, PADDED = 512, 227, 256
GRID, NODES, HALO, SLOTS, DEGREE = 1024, 256, 64, 4, 8
EDGES = NODES * DEGREE
FAR = PEERS * SLOTS


def mm(a, b):
    return lax.dot_general(a, b, (((1,), (0,)), ((), ())), preferred_element_type=F32)


def mmt(a, b):
    return lax.dot_general(a, b, (((1,), (1,)), ((), ())), preferred_element_type=F32)


def tmm(a, b):
    return lax.dot_general(a, b, (((0,), (0,)), ((), ())), preferred_element_type=F32)


def sigmoid(v):
    return 0.5 * jnp.tanh(0.5 * v) + 0.5


def iota(shape, dim):
    return lax.broadcasted_iota(jnp.int32, shape, dim)


def hot(mask):
    return jnp.where(mask, 1.0, 0.0).astype(BF)


def column(row):
    return jnp.transpose(jnp.broadcast_to(row, (8, row.shape[1])))[:, :1]


class Refs:
    def __init__(self, named):
        for name, ref in named.items():
            if isinstance(ref, list):
                ref = [Refs(each) for each in ref]
            setattr(self, name, ref)


GROUPS = (1024, 1536, 1024, 512)


def scratch():
    vm = pltpu.VMEM
    sems = pltpu.SemaphoreType.DMA
    return dict(
        xp=vm((PADDED, GRID), BF),
        cp=vm((PADDED, GRID), BF),
        wep=vm((PADDED, LATENT), BF),
        dwp=vm((PADDED, LATENT), BF),
        grid_ext=vm((GRID + 4 * HALO, LATENT), BF),
        gslope=vm((GRID, LATENT), BF),
        enc_c=vm((NODES, GRID + 4 * HALO), BF),
        enc_t=vm((GRID + 4 * HALO, NODES), BF),
        dec_t=vm((NODES + 4 * HALO, GRID), BF),
        oh_loc=vm((EDGES, NODES), BF),
        oh_far=vm((EDGES, FAR), BF),
        t_loc=vm((NODES, EDGES), BF),
        t_far=vm((FAR, EDGES), BF),
        list_r=vm((FAR, NODES), BF),
        list_t=vm((NODES, FAR), BF),
        p_own=vm((NODES, LATENT), BF),
        p_oth=vm((NODES, LATENT), BF),
        enc_in=vm((NODES, LATENT), BF),
        enc_slope=vm((NODES, LATENT), F32),
        mesh=vm((3, NODES, LATENT), BF),
        agg=vm((2, NODES, LATENT), BF),
        base=vm((EDGES, LATENT), F32),
        slope=vm((EDGES, LATENT), BF),
        ib=vm((EDGES, LATENT), BF),
        rb=vm((NODES, LATENT), BF),
        ab=vm((NODES, LATENT), F32),
        ob=vm((NODES, LATENT), BF),
        lat=vm((NODES, LATENT), F32),
        dback=vm((NODES, PADDED), BF),
        dext=vm((NODES, PADDED), F32),
        sback=vm((NODES, LATENT), F32),
        gback=vm((GRID, LATENT), F32),
        eb=vm((GRID, LATENT), BF),
        far=vm((FAR, LATENT), BF),
        packed=vm((4 * FAR, 128), F32),
        ns0=vm((4 * HALO, LATENT), BF),
        ns1=vm((4 * HALO, PADDED), BF),
        nr1=vm((4 * HALO, PADDED), BF),
        ns2=vm((4 * HALO, LATENT), BF),
        mesh_ext=vm((NODES + 4 * HALO, LATENT), BF),
        ns3=vm((4 * HALO, LATENT), BF),
        nr3=vm((4 * HALO, LATENT), BF),
        near_sem=sems((4, 2)),
        far_sem=sems((4, 2)),
        fars=[dict(source=vm((4 * FAR, 128), BF), target=vm((4 * FAR, 128), BF)) for _ in range(4)],
        groups=[
            dict(
                own=vm((NODES, width), F32),
                sc=vm((NODES, width), BF),
                rc=vm((NODES, width), BF),
                sx=vm((NODES, width), BF),
                rx=vm((192, width), BF),
                fp=vm((width // 2, 128), F32),
                sp=vm((width // 2, 128), BF),
                rp=vm((width // 2, 128), BF),
                sem=sems((3, 2)),
            )
            for width in GROUPS
        ],
    )


def kernel(tree, xt, ct, we, wn, ws, wr, wu, dwt, el, es, ml, ms, dl, ds_, *rest):
    out_pred, out_embed, out_encode, out_source, out_target, out_refresh, out_decode = rest[:7]
    r = Refs(jax.tree.unflatten(tree, rest[7:]))
    ga, gb, gc, gd = r.groups
    b = lax.axis_index("lat")
    c = lax.axis_index("lon")
    me = b * SECTORS + c
    core = lax.rem(c, 2)
    place = c // 2

    barrier = pltpu.get_barrier_semaphore()

    def greet(t, carry):
        u = lax.rem(b + t // SECTORS, BANDS)
        v = lax.rem(c + lax.rem(t, SECTORS), SECTORS)
        pl.semaphore_signal(barrier, inc=1, device_id=(u, v), device_id_type=MESH)
        return carry

    lax.fori_loop(1, PEERS, greet, 0)

    neighbours = (
        (b, lax.rem(c + SECTORS - 1, SECTORS)),
        (b, lax.rem(c + 1, SECTORS)),
        (lax.rem(b + BANDS - 1, BANDS), c),
        (lax.rem(b + 1, BANDS), c),
    )

    def drain(ref, sem):
        pltpu.make_async_copy(ref, ref, sem).wait()

    def near_start(i, source, target):
        for k in range(4):
            pltpu.make_async_remote_copy(
                source.at[pl.ds(k * HALO, HALO)],
                target.at[pl.ds((k ^ 1) * HALO, HALO)],
                r.near_sem.at[i, 0],
                r.near_sem.at[i, 1],
                device_id=neighbours[k],
                device_id_type=MESH,
            ).start()

    def near_wait(i, source, target):
        drain(target, r.near_sem.at[i, 1])
        drain(source, r.near_sem.at[i, 0])

    def far_start(i):
        source, target = r.fars[i].source, r.fars[i].target
        mine = pl.ds(pl.multiple_of(me * 16, 16), 16)

        def send(t, carry):
            u = lax.rem(b + lax.rem(t, BANDS), BANDS)
            v = lax.rem(c + t // BANDS, SECTORS)
            block = pl.ds(pl.multiple_of((u * SECTORS + v) * 16, 16), 16)
            pltpu.make_async_remote_copy(
                source.at[block],
                target.at[mine],
                r.far_sem.at[i, 0],
                r.far_sem.at[i, 1],
                device_id=(u, v),
                device_id_type=MESH,
            ).start()
            return carry

        lax.fori_loop(1, PEERS, send, 0)
        target[mine, :] = source[mine, :]

    def far_wait(i):
        rest_of = pl.ds(0, 16 * (PEERS - 1))
        drain(r.fars[i].target.at[rest_of], r.far_sem.at[i, 1])
        drain(r.fars[i].source.at[rest_of], r.far_sem.at[i, 0])

    packed = r.packed

    def pack(value, target):
        for i in range(SLOTS):
            for j in range(4):
                packed[pl.ds(4 * j + i, PEERS, stride=16), :] = value[
                    i * PEERS : (i + 1) * PEERS, j * 128 : (j + 1) * 128
                ]
        target[...] = packed[...].astype(BF)

    def unpack(source):
        packed[...] = source[...].astype(F32)
        for i in range(SLOTS):
            for j in range(4):
                r.far[i * PEERS : (i + 1) * PEERS, j * 128 : (j + 1) * 128] = packed[
                    pl.ds(4 * j + i, PEERS, stride=16), :
                ].astype(BF)

    def turned(value):
        return (
            mmt(r.p_own[...], value).astype(BF),
            mmt(r.p_oth[...], value).astype(BF),
        )

    def gradient(g, at, width, sides, right, product=mm):
        g.own[:, at : at + width] = product(sides[0], right)
        g.sc[:, at : at + width] = product(sides[1], right).astype(BF)

    def core_start(g):
        pltpu.make_async_remote_copy(
            g.sc,
            g.rc,
            g.sem.at[0, 0],
            g.sem.at[0, 1],
            device_id=(b, c + 1 - 2 * core),
            device_id_type=MESH,
        ).start()

    def core_wait(g):
        drain(g.rc, g.sem.at[0, 1])
        drain(g.sc, g.sem.at[0, 0])
        own, got, out = g.own, g.rc, g.sx
        total = own[...] + got[...].astype(F32)
        own[...] = total
        out[...] = total.astype(BF)

    def band_start(g):
        for t in range(1, BANDS):
            u = lax.rem(b + t, BANDS)
            pltpu.make_async_remote_copy(
                g.sx.at[pl.ds(pl.multiple_of(u * 64, 64), 64)],
                g.rx.at[pl.ds((t - 1) * 64, 64)],
                g.sem.at[1, 0],
                g.sem.at[1, 1],
                device_id=(u, c),
                device_id_type=MESH,
            ).start()

    def band_wait(g):
        drain(g.rx, g.sem.at[1, 1])
        drain(g.sx.at[pl.ds(0, 192)], g.sem.at[1, 0])
        width = g.sc.shape[1]
        rows = width // 32
        got, flat = g.rx, g.fp
        mine = pl.ds(pl.multiple_of(b * 64, 64), 64)
        total = g.own[mine, :]
        for t in range(3):
            total = total + got[t * 64 : (t + 1) * 64, :].astype(F32)
        for j in range(width // 128):
            for i in range(4):
                flat[pl.ds(4 * j + i, 16, stride=rows), :] = total[
                    i * 16 : (i + 1) * 16, j * 128 : (j + 1) * 128
                ]
        g.sp[...] = flat[...].astype(BF)

    def plane_start(g):
        rows = g.sc.shape[1] // 32
        source, target = g.sp, g.rp
        mine = pl.ds(pl.multiple_of(place * rows, 16), rows)

        def send(t, carry):
            q = lax.rem(place + t, 16)
            pltpu.make_async_remote_copy(
                source.at[pl.ds(pl.multiple_of(q * rows, 16), rows)],
                target.at[mine],
                g.sem.at[2, 0],
                g.sem.at[2, 1],
                device_id=(b, q * 2 + core),
                device_id_type=MESH,
            ).start()
            return carry

        lax.fori_loop(1, 16, send, 0)
        target[mine, :] = source[mine, :]

    def plane_wait(g):
        rows = g.sc.shape[1] // 32
        rest_of = pl.ds(0, 15 * rows)
        drain(g.rp.at[rest_of], g.sem.at[2, 1])
        drain(g.sp.at[rest_of], g.sem.at[2, 0])
        got = g.rp
        total = got[0:rows, :].astype(F32)
        for q in range(1, 16):
            total = total + got[q * rows : (q + 1) * rows, :].astype(F32)
        return total

    def deliver(total, at, write):
        for j in range(4):
            row = 4 * (at // 128 + j)
            write(j, total[row : row + 4, :])

    for target, source in ((r.xp, xt), (r.cp, ct), (r.wep, we), (r.dwp, dwt)):
        target[224:256, :] = jnp.zeros((32, source.shape[1]), BF)
        target[0:CHANNELS, :] = source[...]

    def embed(i, carry):
        rows = pl.ds(pl.multiple_of(i * 256, 256), 256)
        inner = tmm(r.xp[:, rows], r.wep[...])
        s = sigmoid(inner)
        value = inner * s
        r.grid_ext[rows, :] = value.astype(BF)
        r.gslope[rows, :] = (s + value * (1.0 - s)).astype(BF)
        return carry

    lax.fori_loop(0, 4, embed, 0)

    def near_row(lists):
        return jnp.concatenate([lists[k : k + 1, :] for k in range(4)], axis=1)

    encode_row = near_row(el)
    decode_row = near_row(dl)
    encode_pick = hot(column(encode_row) == iota((4 * HALO, GRID), 1))
    r.ns0[...] = mm(encode_pick, r.grid_ext[0:GRID, :]).astype(BF)

    pl.semaphore_wait(barrier, PEERS - 1)
    halo_grid = r.grid_ext.at[pl.ds(GRID, 4 * HALO)]
    near_start(0, r.ns0, halo_grid)

    for part in range(2):
        where = iota((NODES, GRID), 0) + part * NODES
        total = jnp.zeros((NODES, GRID), F32)
        for k in range(3):
            total = total + jnp.where(ds_[k : k + 1, :] == where, 1.0, 0.0)
        r.dec_t[part * NODES : (part + 1) * NODES, :] = total.astype(BF)
    r.ns1[...] = mmt(r.dec_t[NODES:, :], r.cp[...]).astype(BF)
    near_start(1, r.ns1, r.nr1)
    r.dext[...] = mmt(r.dec_t[0:NODES, :], r.cp[...])

    es_col = jnp.transpose(es[...])
    for part in range(5):
        where = iota((NODES, 256), 1) + part * 256
        where_t = iota((256, NODES), 0) + part * 256
        total = jnp.zeros((NODES, 256), F32)
        total_t = jnp.zeros((256, NODES), F32)
        for k in range(DEGREE):
            total = total + jnp.where(es_col[:, k : k + 1] == where, 1.0, 0.0)
            total_t = total_t + jnp.where(es[k : k + 1, :] == where_t, 1.0, 0.0)
        r.enc_c[:, part * 256 : (part + 1) * 256] = total.astype(BF)
        r.enc_t[part * 256 : (part + 1) * 256, :] = total_t.astype(BF)
    encode_local = mm(r.enc_c[:, 0:GRID], r.grid_ext[0:GRID, :])

    for i in range(SLOTS):
        row = ml[i : i + 1, :]
        r.list_r[i * PEERS : (i + 1) * PEERS, :] = hot(column(row) == iota((PEERS, NODES), 1))
        r.list_t[:, i * PEERS : (i + 1) * PEERS] = hot(row == iota((NODES, PEERS), 0))

    near_wait(0, r.ns0, halo_grid)
    encode_input = (encode_local + mm(r.enc_c[:, GRID:], r.grid_ext[GRID:, :])).astype(BF)
    r.enc_in[...] = encode_input
    encode_inner = mm(encode_input, wn[...])
    s = sigmoid(encode_inner)
    value = encode_inner * s
    r.mesh[0] = value.astype(BF)
    r.enc_slope[...] = s + value * (1.0 - s)

    def send_rows(layer):
        sender = mm(r.mesh[layer], ws[layer]).astype(BF)
        pack(mm(r.list_r[...], sender), r.fars[layer].source)
        far_start(layer)
        return sender

    def local_rows(layer, sender):
        receiver = mm(r.mesh[layer], wr[layer])
        for k in range(DEGREE):
            rows = slice(k * NODES, (k + 1) * NODES)
            r.base[rows, :] = mm(r.oh_loc[rows, :], sender) + receiver

    def far_rows(layer):
        far_wait(layer)
        unpack(r.fars[layer].target)

        def add(k, carry):
            rows = pl.ds(pl.multiple_of(k * NODES, NODES), NODES)
            r.base[rows, :] += mm(r.oh_far[rows, :], r.far[...])
            return carry

        lax.fori_loop(0, DEGREE, add, 0)

    sender = send_rows(0)

    def far_index(v):
        k = v - NODES
        return jnp.where(k >= 0, (k & 3) * PEERS + (k >> 2), -1)

    ms_row = ms[...]
    ms_col = jnp.transpose(ms_row)
    far_row = far_index(ms_row)
    far_col = far_index(ms_col)
    for k in range(DEGREE):
        rows = slice(k * NODES, (k + 1) * NODES)
        r.oh_loc[rows, :] = hot(ms_col[:, k : k + 1] == iota((NODES, NODES), 1))
        r.oh_far[rows, :] = hot(far_col[:, k : k + 1] == iota((NODES, FAR), 1))
        r.t_loc[:, rows] = hot(ms_row[k : k + 1, :] == iota((NODES, NODES), 0))
        r.t_far[:, rows] = hot(far_row[k : k + 1, :] == iota((FAR, NODES), 0))
    local_rows(0, sender)

    index = iota((NODES, LATENT), 0)
    first = (index // 64) * 128 + (index % 16) * 8 + (index // 16) % 4
    r.p_own[...] = hot(first + core * 4 == iota((NODES, LATENT), 1))
    r.p_oth[...] = hot(first + (1 - core) * 4 == iota((NODES, LATENT), 1))

    decode_spread = hot(decode_row == iota((NODES, 4 * HALO), 0))
    near_wait(1, r.ns1, r.nr1)
    decode_back = (r.dext[...] + mm(decode_spread, r.nr1[...])).astype(BF)
    r.dback[...] = decode_back
    latent_back = mm(decode_back, r.dwp[...])
    r.lat[...] = latent_back
    out_back = latent_back.astype(BF)
    r.ob[...] = out_back
    r.ab[...] = mmt(out_back, wu[1])

    far_rows(0)
    chunk = 32

    def edges_0(i, carry):
        at = pl.multiple_of(i * chunk, chunk)
        total = jnp.zeros((chunk, LATENT), F32)
        for k in range(DEGREE):
            rows = pl.ds(k * NODES + at, chunk)
            inner = r.base[rows, :]
            s = sigmoid(inner)
            value = inner * s
            total = total + value
            r.slope[rows, :] = (s + value * (1.0 - s)).astype(BF)
        r.agg[0, pl.ds(at, chunk), :] = total.astype(BF)
        return carry

    lax.fori_loop(0, NODES // chunk, edges_0, 0)
    r.mesh[1] = (r.mesh[0].astype(F32) + mm(r.agg[0], wu[0])).astype(BF)

    sender = send_rows(1)
    local_rows(1, sender)
    far_rows(1)

    def edges_1(i, carry):
        at = pl.multiple_of(i * chunk, chunk)
        total = jnp.zeros((chunk, LATENT), F32)
        back = jnp.zeros((chunk, LATENT), F32)
        given = r.ab[pl.ds(at, chunk), :]
        for k in range(DEGREE):
            rows = pl.ds(k * NODES + at, chunk)
            inner = r.base[rows, :]
            s = sigmoid(inner)
            value = inner * s
            total = total + value
            edge = given * (s + value * (1.0 - s))
            back = back + edge
            r.ib[rows, :] = edge.astype(BF)
        r.agg[1, pl.ds(at, chunk), :] = total.astype(BF)
        r.rb[pl.ds(at, chunk), :] = back.astype(BF)
        return carry

    lax.fori_loop(0, NODES // chunk, edges_1, 0)

    def edges_back(i, carry):
        at = pl.multiple_of(i * chunk, chunk)
        back = jnp.zeros((chunk, LATENT), F32)
        given = r.ab[pl.ds(at, chunk), :]
        for k in range(DEGREE):
            rows = pl.ds(k * NODES + at, chunk)
            edge = given * r.slope[rows, :].astype(F32)
            back = back + edge
            r.ib[rows, :] = edge.astype(BF)
        r.rb[pl.ds(at, chunk), :] = back.astype(BF)
        return carry

    def return_start(slot):
        pack(mm(r.t_far[...], r.ib[...]), r.fars[slot].source)
        far_start(slot)

    def return_local(layer):
        r.sback[...] = mm(r.t_loc[...], r.ib[...])
        r.lat[...] += mmt(r.rb[...], wr[layer])

    def return_end(slot, layer):
        far_wait(slot)
        unpack(r.fars[slot].target)
        sender_b = (r.sback[...] + mm(r.list_t[...], r.far[...])).astype(BF)
        r.lat[...] += mmt(sender_b, ws[layer])
        return sender_b

    return_start(2)
    mesh_last = (r.mesh[1].astype(F32) + mm(r.agg[1], wu[1])).astype(BF)
    r.mesh[2] = mesh_last
    r.mesh_ext[0:NODES, :] = mesh_last
    decode_pick = hot(column(decode_row) == iota((4 * HALO, NODES), 1))
    r.ns2[...] = mm(decode_pick, mesh_last).astype(BF)
    halo_mesh = r.mesh_ext.at[pl.ds(NODES, 4 * HALO)]
    near_start(2, r.ns2, halo_mesh)
    return_local(1)
    gradient(gd, 0, 256, turned(mesh_last), r.dback[...])
    gradient(ga, 0, 512, turned(r.ob[...]), r.agg[1])
    gradient(ga, 512, 512, turned(r.rb[...]), r.mesh[1])
    core_start(ga)
    near_wait(2, r.ns2, halo_mesh)
    sender_b1 = return_end(2, 1)

    out_back = r.lat[...].astype(BF)
    r.ob[...] = out_back
    r.ab[...] = mmt(out_back, wu[0])
    lax.fori_loop(0, NODES // chunk, edges_back, 0)
    return_start(3)
    core_wait(ga)
    band_start(ga)
    return_local(0)
    gradient(gb, 0, 512, turned(sender_b1), r.mesh[1])
    gradient(gb, 512, 512, turned(r.ob[...]), r.agg[0])
    gradient(gb, 1024, 512, turned(r.rb[...]), r.mesh[0])
    core_start(gb)
    decoded = mmt(r.dwp[...], r.mesh_ext[...]).astype(BF)
    forecast = r.xp[...].astype(F32) + mm(decoded, r.dec_t[...])
    out_pred[...] = forecast[0:CHANNELS, :].astype(BF)
    band_wait(ga)
    plane_start(ga)
    sender_b0 = return_end(3, 0)

    encode_back = (r.lat[...] * r.enc_slope[...]).astype(BF)
    input_back = mmt(encode_back, wn[...]).astype(BF)
    r.ns3[...] = mm(r.enc_t[GRID:, :], input_back).astype(BF)
    near_start(3, r.ns3, r.nr3)
    core_wait(gb)
    band_start(gb)
    r.gback[...] = mm(r.enc_t[0:GRID, :], input_back)
    gradient(gc, 0, 512, turned(sender_b0), r.mesh[0])
    gradient(gc, 512, 512, turned(encode_back), r.enc_in[...])
    core_start(gc)
    encode_spread = hot(encode_row == iota((GRID, 4 * HALO), 0))
    near_wait(3, r.ns3, r.nr3)
    r.gback[...] += mm(encode_spread, r.nr3[...])
    r.eb[...] = (r.gback[...] * r.gslope[...].astype(F32)).astype(BF)
    gradient(gd, 256, 256, turned(r.eb[...]), r.xp[...], mmt)
    core_start(gd)
    core_wait(gc)
    band_start(gc)
    core_wait(gd)
    band_start(gd)

    total = plane_wait(ga)

    def into(ref, layer=None):
        def write(j, value):
            if layer is None:
                ref[:, j * 128 : (j + 1) * 128] = value
            else:
                ref[layer, :, j * 128 : (j + 1) * 128] = value

        return write

    deliver(total, 0, into(out_refresh, 1))
    deliver(total, 512, into(out_target, 1))
    band_wait(gb)
    plane_start(gb)
    band_wait(gc)
    plane_start(gc)
    band_wait(gd)
    plane_start(gd)
    total = plane_wait(gb)
    deliver(total, 0, into(out_source, 1))
    deliver(total, 512, into(out_refresh, 0))
    deliver(total, 1024, into(out_target, 0))
    total = plane_wait(gc)
    deliver(total, 0, into(out_source, 0))
    deliver(total, 512, into(out_encode))
    total = plane_wait(gd)
    for ref, row in ((out_decode, 0), (out_embed, 8)):
        ref[:, 0:128] = total[row : row + 4, :]
        ref[:, 128:CHANNELS] = total[row + 4 : row + 8, 0 : CHANNELS - 128]


def on_device(
    lattice_feature_values,
    cotangent,
    embed_weight,
    encode_weight,
    sender_weight,
    receiver_weight,
    update_weight,
    decode_weight,
    encode_lists,
    encode_sources,
    mesh_lists,
    mesh_sources,
    decode_lists,
    decoder_edge_sources,
):
    spec, tree = jax.tree.flatten(scratch())
    whole = pl.BlockSpec(memory_space=pltpu.VMEM)
    shape = jax.ShapeDtypeStruct
    outs = pl.pallas_call(
        functools.partial(kernel, tree),
        out_shape=(
            shape((CHANNELS, GRID), BF),
            shape((4, CHANNELS), F32),
            shape((4, LATENT), F32),
            shape((2, 4, LATENT), F32),
            shape((2, 4, LATENT), F32),
            shape((2, 4, LATENT), F32),
            shape((4, CHANNELS), F32),
        ),
        in_specs=[whole] * 14,
        out_specs=(whole,) * 7,
        scratch_shapes=spec,
        compiler_params=pltpu.CompilerParams(
            collective_id=0, has_side_effects=True, vmem_limit_bytes=60 * 1024 * 1024
        ),
    )(
        lattice_feature_values.T,
        cotangent.T,
        embed_weight,
        encode_weight,
        sender_weight,
        receiver_weight,
        update_weight,
        decode_weight.T,
        encode_lists,
        encode_sources.T,
        mesh_lists.T,
        mesh_sources.T,
        decode_lists,
        decoder_edge_sources.T,
    )
    return (
        outs[0].T,
        outs[1].T,
        outs[2].T,
        outs[3].transpose(0, 2, 1),
        outs[4].transpose(0, 2, 1),
        outs[5].transpose(0, 2, 1),
        outs[6],
    )


def solution(mesh):
    return jax.shard_map(
        on_device,
        mesh=mesh,
        in_specs=(
            P(("lat", "lon"), None),
            P(("lat", "lon"), None),
            P(),
            P(),
            P(),
            P(),
            P(),
            P(),
            P(("lat", "lon"), None),
            P(("lat", "lon"), None),
            P(("lat", "lon"), None),
            P(("lat", "lon"), None),
            P(("lat", "lon"), None),
            P(("lat", "lon"), None),
        ),
        out_specs=(
            P(("lat", "lon"), None),
            P(None, ("lat", "lon")),
            P(None, ("lat", "lon")),
            P(None, None, ("lat", "lon")),
            P(None, None, ("lat", "lon")),
            P(None, None, ("lat", "lon")),
            P(("lat", "lon"), None),
        ),
        check_vma=False,
    )
```

time: 402 us -> 113 us (0.28); the launches traced: 395 us -> 112 us
  waiting for transfers between devices: 183 us -> 0 us
  Pallas kernels: 0 us -> 106 us
  matrix products: 68.6 us -> 0 us
  starting transfers between devices: 63 us -> 0 us
  local copies, waits for them, and re-layouts: 60.9 us -> 5.76 us
  between operations: 16.3 us -> 0.67 us
    unnamed x2 -> x0, waiting for transfers between devices: 143 us -> none
    pallas_call x0 -> x1, Pallas kernels: none -> 106 us  [on_device(): pl.pallas_call(functools.partial(kernel, tree), out_shape=(shape((CHANNEL...]
    dot_general x69 -> x0, matrix products: 68.6 us -> none  [the longest x51 47.6 us: left_product(): lax.dot_general(first, second, (((0,), (0,)), ((), ())), preferred_elemen...]
    ppermute x16 -> x0, starting transfers between devices: 39.3 us -> none  [the longest x8 21.5 us: shifted(): lax.ppermute(value, axis, [(i, (i + by) % length) for i in range(length)])]
    all_to_all x4 -> x0, waiting for transfers between devices: 30.5 us -> none  [the longest x2 20.9 us: pass_rows(): lax.all_to_all(payload, ('lat', 'lon'), split_axis=0, concat_axis=0, tile...]
    all_to_all x4 -> x0, starting transfers between devices: 23.4 us -> none  [the longest x2 11.8 us: return_rows(): lax.all_to_all(outgoing.astype(jnp.bfloat16), ('lat', 'lon'), split_axis=...]
    gather x6 -> x0, local copies, waits for them, and re-layouts: 21.6 us -> none  [the longest x2 15.1 us: on_device(): fetched = sender_ext[mesh_sources]]
    ppermute x16 -> x0, waiting for transfers between devices: 9.63 us -> none  [the longest x8 9.61 us: shifted_2(): return lax.ppermute(block, axis, route)]
  transfers between devices with their start and end apart: 21 -> 0, of which waited for: 9 -> 0; matrix products, arithmetic and copies ran while one was open for 10% -> 0% of each run, Pallas kernels for 0% -> 0%
where the time goes in v1:
time: 113 us; the launch traced here: 112 us
  Pallas kernels  106 us (94%)
  local copies, waits for them, and re-layouts  5.76 us (5%)
    pallas_call x1, Pallas kernels, on_device(): pl.pallas_call(functools.partial(kernel, tree), out_shape=(shape((CHANNEL...  106 us
    unnamed x19, local copies, waits for them, and re-layouts  5.76 us

profile of v1, /device:TPU:0, one launch (start us, length us, event | category | flops | bytes accessed | tf_op | source)
XLA Modules:
  0.0 112.5 jit_solution(136940440729019738)
XLA Ops:
  0.6 106.0 %shard_map.189 = (bf16[227,1024]{1,0:T(8,128)(2,1)}, f32[4,227]{1,0:T(4,128)}, f32[4,512]{1,0:T(4,128)}, f32[2,4,512]{2,1,0:T(4,128)}, f32[2,4,512]{2,1,0:T(4,12...) custom-call(bf16[227,1024]{1,0:T(8,128)(2,1)} %bitcast.14, bf16[227,1024]{1,0:T(8,128)(2,1)} %bitcast.15, ...), custom_call_target="tpu_custom_call" | custom-call | tf_op jit(solution)/shard_map/pallas_call | solution.py:605
  106.7 0.0 copy-start.5
  106.7 0.0 copy-start.3
  106.7 1.8 %copy.28 = bf16[1024,227]{0,1:T(8,128)(2,1)} copy(bf16[1024,227]{0,1:T(8,128)(2,1)} %bitcast.13) | data formatting | bytes 929792
  108.5 0.0 copy-done.5
  108.5 0.0 copy-start.2
  108.5 0.6 copy.29
  109.1 0.0 copy-done.3
  109.1 0.6 copy.30
  109.7 0.0 copy-done.2
  109.7 0.0 copy-start.1
  109.7 0.6 copy.31
  110.3 0.1 copy-done.1
  110.5 0.0 copy-start
  110.5 0.6 copy.32
  111.1 0.1 copy-done
  111.2 0.0 copy-start.4
  111.2 0.6 copy.33
  111.8 0.1 copy-done.4
  111.9 0.6 copy.34
Async XLA Ops:
  106.7 1.9 %copy-start.5 = (f32[4,227]{1,0:T(4,128)S(1)}, f32[4,227]{1,0:T(4,128)}, u32[]{:S(2)}) copy-start(f32[4,227]{1,0:T(4,128)} %get-tuple-element.15) | copy-start | bytes 10900
  106.7 2.4 %copy-start.3 = (f32[4,512]{1,0:T(4,128)S(1)}, f32[4,512]{1,0:T(4,128)}, u32[]{:S(2)}) copy-start(f32[4,512]{1,0:T(4,128)} %get-tuple-element.16) | copy-start | bytes 24580
  108.5 1.2 %copy-start.2 = (f32[2,4,512]{2,1,0:T(4,128)S(1)}, f32[2,4,512]{2,1,0:T(4,128)}, u32[]{:S(2)}) copy-start(f32[2,4,512]{2,1,0:T(4,128)} %get-tuple-element.17) | copy-start | bytes 49156
  109.7 0.7 copy-start.1
  110.5 0.7 copy-start
  111.2 0.7 copy-start.4

commit v2 on v1

--- a/solution.py
+++ b/solution.py
@@ -54,7 +54,7 @@
             setattr(self, name, ref)
 
 
-GROUPS = (1024, 1536, 1024, 512)
+GROUPS = ((512, True), (512, False), (1024, True), (512, False), (512, True), (512, False), (512, True))
 
 
 def scratch():
@@ -76,13 +76,13 @@
         t_far=vm((FAR, EDGES), BF),
         list_r=vm((FAR, NODES), BF),
         list_t=vm((NODES, FAR), BF),
-        p_own=vm((NODES, LATENT), BF),
-        p_oth=vm((NODES, LATENT), BF),
+        p_own=vm((2, NODES, LATENT), BF),
+        p_oth=vm((2, NODES, LATENT), BF),
         enc_in=vm((NODES, LATENT), BF),
         enc_slope=vm((NODES, LATENT), F32),
         mesh=vm((3, NODES, LATENT), BF),
         agg=vm((2, NODES, LATENT), BF),
-        base=vm((EDGES, LATENT), F32),
+        base=vm((2, EDGES, LATENT), F32),
         slope=vm((EDGES, LATENT), BF),
         ib=vm((EDGES, LATENT), BF),
         rb=vm((NODES, LATENT), BF),
@@ -112,13 +112,13 @@
                 sc=vm((NODES, width), BF),
                 rc=vm((NODES, width), BF),
                 sx=vm((NODES, width), BF),
-                rx=vm((192, width), BF),
-                fp=vm((width // 2, 128), F32),
-                sp=vm((width // 2, 128), BF),
-                rp=vm((width // 2, 128), BF),
+                rx=vm((192 if along else NODES, width), BF),
+                fp=vm((width // 2 if along else width // 8, 128), F32),
+                sp=vm((width // 2 if along else width // 8, 128), BF),
+                rp=vm((width // 2 if along else 3 * width // 32, 128), BF),
                 sem=sems((3, 2)),
             )
-            for width in GROUPS
+            for width, along in GROUPS
         ],
     )
 
@@ -126,7 +126,9 @@
 def kernel(tree, xt, ct, we, wn, ws, wr, wu, dwt, el, es, ml, ms, dl, ds_, *rest):
     out_pred, out_embed, out_encode, out_source, out_target, out_refresh, out_decode = rest[:7]
     r = Refs(jax.tree.unflatten(tree, rest[7:]))
-    ga, gb, gc, gd = r.groups
+    for each, (width, along) in zip(r.groups, GROUPS):
+        each.along = along
+    g_u1, g_r1, g_su, g_r0, g_s0, g_en, g_de = r.groups
     b = lax.axis_index("lat")
     c = lax.axis_index("lon")
     me = b * SECTORS + c
@@ -212,15 +214,18 @@
                     pl.ds(4 * j + i, PEERS, stride=16), :
                 ].astype(BF)
 
-    def turned(value):
+    def turned(g, value):
+        order = 0 if g.along else 1
         return (
-            mmt(r.p_own[...], value).astype(BF),
-            mmt(r.p_oth[...], value).astype(BF),
+            mmt(r.p_own[order], value).astype(BF),
+            mmt(r.p_oth[order], value).astype(BF),
         )
 
-    def gradient(g, at, width, sides, right, product=mm):
-        g.own[:, at : at + width] = product(sides[0], right)
-        g.sc[:, at : at + width] = product(sides[1], right).astype(BF)
+    def gradient(g, at, left, right):
+        width = right.shape[1]
+        sides = turned(g, left)
+        g.own[:, at : at + width] = mm(sides[0], right)
+        g.sc[:, at : at + width] = mm(sides[1], right).astype(BF)
 
     def core_start(g):
         pltpu.make_async_remote_copy(
@@ -235,43 +240,23 @@
     def core_wait(g):
         drain(g.rc, g.sem.at[0, 1])
         drain(g.sc, g.sem.at[0, 0])
-        own, got, out = g.own, g.rc, g.sx
-        total = own[...] + got[...].astype(F32)
-        own[...] = total
-        out[...] = total.astype(BF)
-
-    def band_start(g):
+        total = g.own[...] + g.rc[...].astype(F32)
+        g.own[...] = total
+        g.sx[...] = total.astype(BF)
+
+    def over_bands(g, hop, source, target, rows):
         for t in range(1, BANDS):
             u = lax.rem(b + t, BANDS)
             pltpu.make_async_remote_copy(
-                g.sx.at[pl.ds(pl.multiple_of(u * 64, 64), 64)],
-                g.rx.at[pl.ds((t - 1) * 64, 64)],
-                g.sem.at[1, 0],
-                g.sem.at[1, 1],
+                source.at[pl.ds(pl.multiple_of(u * rows, 16), rows)],
+                target.at[pl.ds((t - 1) * rows, rows)],
+                g.sem.at[hop, 0],
+                g.sem.at[hop, 1],
                 device_id=(u, c),
                 device_id_type=MESH,
             ).start()
 
-    def band_wait(g):
-        drain(g.rx, g.sem.at[1, 1])
-        drain(g.sx.at[pl.ds(0, 192)], g.sem.at[1, 0])
-        width = g.sc.shape[1]
-        rows = width // 32
-        got, flat = g.rx, g.fp
-        mine = pl.ds(pl.multiple_of(b * 64, 64), 64)
-        total = g.own[mine, :]
-        for t in range(3):
-            total = total + got[t * 64 : (t + 1) * 64, :].astype(F32)
-        for j in range(width // 128):
-            for i in range(4):
-                flat[pl.ds(4 * j + i, 16, stride=rows), :] = total[
-                    i * 16 : (i + 1) * 16, j * 128 : (j + 1) * 128
-                ]
-        g.sp[...] = flat[...].astype(BF)
-
-    def plane_start(g):
-        rows = g.sc.shape[1] // 32
-        source, target = g.sp, g.rp
+    def over_plane(g, hop, source, target, rows):
         mine = pl.ds(pl.multiple_of(place * rows, 16), rows)
 
         def send(t, carry):
@@ -279,8 +264,8 @@
             pltpu.make_async_remote_copy(
                 source.at[pl.ds(pl.multiple_of(q * rows, 16), rows)],
                 target.at[mine],
-                g.sem.at[2, 0],
-                g.sem.at[2, 1],
+                g.sem.at[hop, 0],
+                g.sem.at[hop, 1],
                 device_id=(b, q * 2 + core),
                 device_id_type=MESH,
             ).start()
@@ -289,16 +274,57 @@
         lax.fori_loop(1, 16, send, 0)
         target[mine, :] = source[mine, :]
 
-    def plane_wait(g):
+    def plane_sum(g, hop, source, target, rows):
+        rest_of = pl.ds(0, 15 * rows)
+        drain(target.at[rest_of], g.sem.at[hop, 1])
+        drain(source.at[rest_of], g.sem.at[hop, 0])
+        total = target[0:rows, :].astype(F32)
+        for q in range(1, 16):
+            total = total + target[q * rows : (q + 1) * rows, :].astype(F32)
+        return total
+
+    def band_sum(g, hop, source, target, rows, own):
+        drain(target, g.sem.at[hop, 1])
+        drain(source.at[pl.ds(0, 3 * rows)], g.sem.at[hop, 0])
+        total = own[pl.ds(pl.multiple_of(b * rows, 8), rows), :]
+        for t in range(3):
+            total = total + target[t * rows : (t + 1) * rows, :].astype(F32)
+        return total
+
+    def first_start(g):
+        core_wait(g)
+        if g.along:
+            over_bands(g, 1, g.sx, g.rx, 64)
+        else:
+            over_plane(g, 1, g.sx, g.rx, 16)
+
+    def second_start(g):
+        width = g.sc.shape[1]
+        rows = width // 32
+        if g.along:
+            total = band_sum(g, 1, g.sx, g.rx, 64, g.own)
+            for j in range(width // 128):
+                for i in range(4):
+                    g.fp[pl.ds(4 * j + i, 16, stride=rows), :] = total[
+                        i * 16 : (i + 1) * 16, j * 128 : (j + 1) * 128
+                    ]
+        else:
+            total = plane_sum(g, 1, g.sx, g.rx, 16)
+            for u in range(4):
+                for j in range(width // 128):
+                    at = u * rows + 4 * j
+                    g.fp[at : at + 4, :] = total[u * 4 : (u + 1) * 4, j * 128 : (j + 1) * 128]
+        g.sp[...] = g.fp[...].astype(BF)
+        if g.along:
+            over_plane(g, 2, g.sp, g.rp, rows)
+        else:
+            over_bands(g, 2, g.sp, g.rp, rows)
+
+    def finish(g):
         rows = g.sc.shape[1] // 32
-        rest_of = pl.ds(0, 15 * rows)
-        drain(g.rp.at[rest_of], g.sem.at[2, 1])
-        drain(g.sp.at[rest_of], g.sem.at[2, 0])
-        got = g.rp
-        total = got[0:rows, :].astype(F32)
-        for q in range(1, 16):
-            total = total + got[q * rows : (q + 1) * rows, :].astype(F32)
-        return total
+        if g.along:
+            return plane_sum(g, 2, g.sp, g.rp, rows)
+        return band_sum(g, 2, g.sp, g.rp, rows, g.fp)
 
     def deliver(total, at, write):
         for j in range(4):
@@ -331,6 +357,67 @@
     pl.semaphore_wait(barrier, PEERS - 1)
     halo_grid = r.grid_ext.at[pl.ds(GRID, 4 * HALO)]
     near_start(0, r.ns0, halo_grid)
+
+    es_col = jnp.transpose(es[...])
+    for part in range(5):
+        where = iota((NODES, 256), 1) + part * 256
+        total = jnp.zeros((NODES, 256), F32)
+        for k in range(DEGREE):
+            total = total + jnp.where(es_col[:, k : k + 1] == where, 1.0, 0.0)
+        r.enc_c[:, part * 256 : (part + 1) * 256] = total.astype(BF)
+    encode_local = mm(r.enc_c[:, 0:GRID], r.grid_ext[0:GRID, :])
+
+    for i in range(SLOTS):
+        row = ml[i : i + 1, :]
+        r.list_r[i * PEERS : (i + 1) * PEERS, :] = hot(column(row) == iota((PEERS, NODES), 1))
+
+    near_wait(0, r.ns0, halo_grid)
+    encode_input = (encode_local + mm(r.enc_c[:, GRID:], r.grid_ext[GRID:, :])).astype(BF)
+    r.enc_in[...] = encode_input
+    encode_inner = mm(encode_input, wn[...])
+    s = sigmoid(encode_inner)
+    value = encode_inner * s
+    r.mesh[0] = value.astype(BF)
+    r.enc_slope[...] = s + value * (1.0 - s)
+
+    def send_rows(layer):
+        sender = mm(r.mesh[layer], ws[layer]).astype(BF)
+        pack(mm(r.list_r[...], sender), r.fars[layer].source)
+        far_start(layer)
+        return sender
+
+    def local_rows(layer, sender):
+        receiver = mm(r.mesh[layer], wr[layer])
+        for k in range(DEGREE):
+            rows = slice(k * NODES, (k + 1) * NODES)
+            r.base[layer, rows, :] = mm(r.oh_loc[rows, :], sender) + receiver
+
+    def far_rows(layer):
+        far_wait(layer)
+        unpack(r.fars[layer].target)
+
+        def add(k, carry):
+            rows = pl.ds(pl.multiple_of(k * NODES, NODES), NODES)
+            r.base[layer, rows, :] += mm(r.oh_far[rows, :], r.far[...])
+            return carry
+
+        lax.fori_loop(0, DEGREE, add, 0)
+
+    sender = send_rows(0)
+
+    def far_index(v):
+        k = v - NODES
+        return jnp.where(k >= 0, (k & 3) * PEERS + (k >> 2), -1)
+
+    ms_row = ms[...]
+    ms_col = jnp.transpose(ms_row)
+    far_row = far_index(ms_row)
+    far_col = far_index(ms_col)
+    for k in range(DEGREE):
+        rows = slice(k * NODES, (k + 1) * NODES)
+        r.oh_loc[rows, :] = hot(ms_col[:, k : k + 1] == iota((NODES, NODES), 1))
+        r.oh_far[rows, :] = hot(far_col[:, k : k + 1] == iota((NODES, FAR), 1))
+    local_rows(0, sender)
 
     for part in range(2):
         where = iota((NODES, GRID), 0) + part * NODES
@@ -342,78 +429,23 @@
     near_start(1, r.ns1, r.nr1)
     r.dext[...] = mmt(r.dec_t[0:NODES, :], r.cp[...])
 
-    es_col = jnp.transpose(es[...])
-    for part in range(5):
-        where = iota((NODES, 256), 1) + part * 256
-        where_t = iota((256, NODES), 0) + part * 256
-        total = jnp.zeros((NODES, 256), F32)
-        total_t = jnp.zeros((256, NODES), F32)
+    far_rows(0)
+    chunk = 32
+
+    def edges_0(i, carry):
+        at = pl.multiple_of(i * chunk, chunk)
+        total = jnp.zeros((chunk, LATENT), F32)
         for k in range(DEGREE):
-            total = total + jnp.where(es_col[:, k : k + 1] == where, 1.0, 0.0)
-            total_t = total_t + jnp.where(es[k : k + 1, :] == where_t, 1.0, 0.0)
-        r.enc_c[:, part * 256 : (part + 1) * 256] = total.astype(BF)
-        r.enc_t[part * 256 : (part + 1) * 256, :] = total_t.astype(BF)
-    encode_local = mm(r.enc_c[:, 0:GRID], r.grid_ext[0:GRID, :])
-
-    for i in range(SLOTS):
-        row = ml[i : i + 1, :]
-        r.list_r[i * PEERS : (i + 1) * PEERS, :] = hot(column(row) == iota((PEERS, NODES), 1))
-        r.list_t[:, i * PEERS : (i + 1) * PEERS] = hot(row == iota((NODES, PEERS), 0))
-
-    near_wait(0, r.ns0, halo_grid)
-    encode_input = (encode_local + mm(r.enc_c[:, GRID:], r.grid_ext[GRID:, :])).astype(BF)
-    r.enc_in[...] = encode_input
-    encode_inner = mm(encode_input, wn[...])
-    s = sigmoid(encode_inner)
-    value = encode_inner * s
-    r.mesh[0] = value.astype(BF)
-    r.enc_slope[...] = s + value * (1.0 - s)
-
-    def send_rows(layer):
-        sender = mm(r.mesh[layer], ws[layer]).astype(BF)
-        pack(mm(r.list_r[...], sender), r.fars[layer].source)
-        far_start(layer)
-        return sender
-
-    def local_rows(layer, sender):
-        receiver = mm(r.mesh[layer], wr[layer])
-        for k in range(DEGREE):
-            rows = slice(k * NODES, (k + 1) * NODES)
-            r.base[rows, :] = mm(r.oh_loc[rows, :], sender) + receiver
-
-    def far_rows(layer):
-        far_wait(layer)
-        unpack(r.fars[layer].target)
-
-        def add(k, carry):
-            rows = pl.ds(pl.multiple_of(k * NODES, NODES), NODES)
-            r.base[rows, :] += mm(r.oh_far[rows, :], r.far[...])
-            return carry
-
-        lax.fori_loop(0, DEGREE, add, 0)
-
-    sender = send_rows(0)
-
-    def far_index(v):
-        k = v - NODES
-        return jnp.where(k >= 0, (k & 3) * PEERS + (k >> 2), -1)
-
-    ms_row = ms[...]
-    ms_col = jnp.transpose(ms_row)
-    far_row = far_index(ms_row)
-    far_col = far_index(ms_col)
-    for k in range(DEGREE):
-        rows = slice(k * NODES, (k + 1) * NODES)
-        r.oh_loc[rows, :] = hot(ms_col[:, k : k + 1] == iota((NODES, NODES), 1))
-        r.oh_far[rows, :] = hot(far_col[:, k : k + 1] == iota((NODES, FAR), 1))
-        r.t_loc[:, rows] = hot(ms_row[k : k + 1, :] == iota((NODES, NODES), 0))
-        r.t_far[:, rows] = hot(far_row[k : k + 1, :] == iota((FAR, NODES), 0))
-    local_rows(0, sender)
-
-    index = iota((NODES, LATENT), 0)
-    first = (index // 64) * 128 + (index % 16) * 8 + (index // 16) % 4
-    r.p_own[...] = hot(first + core * 4 == iota((NODES, LATENT), 1))
-    r.p_oth[...] = hot(first + (1 - core) * 4 == iota((NODES, LATENT), 1))
+            inner = r.base[0, pl.ds(k * NODES + at, chunk), :]
+            total = total + inner * sigmoid(inner)
+        r.agg[0, pl.ds(at, chunk), :] = total.astype(BF)
+        return carry
+
+    lax.fori_loop(0, NODES // chunk, edges_0, 0)
+    r.mesh[1] = (r.mesh[0].astype(F32) + mm(r.agg[0], wu[0])).astype(BF)
+
+    sender = send_rows(1)
+    local_rows(1, sender)
 
     decode_spread = hot(decode_row == iota((NODES, 4 * HALO), 0))
     near_wait(1, r.ns1, r.nr1)
@@ -425,27 +457,30 @@
     r.ob[...] = out_back
     r.ab[...] = mmt(out_back, wu[1])
 
-    far_rows(0)
-    chunk = 32
-
-    def edges_0(i, carry):
-        at = pl.multiple_of(i * chunk, chunk)
-        total = jnp.zeros((chunk, LATENT), F32)
-        for k in range(DEGREE):
-            rows = pl.ds(k * NODES + at, chunk)
-            inner = r.base[rows, :]
-            s = sigmoid(inner)
-            value = inner * s
-            total = total + value
-            r.slope[rows, :] = (s + value * (1.0 - s)).astype(BF)
-        r.agg[0, pl.ds(at, chunk), :] = total.astype(BF)
+    def slopes(i, carry):
+        rows = pl.ds(pl.multiple_of(i * 64, 64), 64)
+        inner = r.base[0, rows, :]
+        s = sigmoid(inner)
+        r.slope[rows, :] = (s + inner * s * (1.0 - s)).astype(BF)
         return carry
 
-    lax.fori_loop(0, NODES // chunk, edges_0, 0)
-    r.mesh[1] = (r.mesh[0].astype(F32) + mm(r.agg[0], wu[0])).astype(BF)
-
-    sender = send_rows(1)
-    local_rows(1, sender)
+    lax.fori_loop(0, EDGES // 64, slopes, 0)
+    for k in range(DEGREE):
+        rows = slice(k * NODES, (k + 1) * NODES)
+        r.t_loc[:, rows] = hot(ms_row[k : k + 1, :] == iota((NODES, NODES), 0))
+        r.t_far[:, rows] = hot(far_row[k : k + 1, :] == iota((FAR, NODES), 0))
+    for i in range(SLOTS):
+        row = ml[i : i + 1, :]
+        r.list_t[:, i * PEERS : (i + 1) * PEERS] = hot(row == iota((NODES, PEERS), 0))
+
+    index = iota((NODES, LATENT), 0)
+    named = iota((NODES, LATENT), 1)
+    by_band = (index // 64) * 128 + (index % 16) * 8 + (index // 16) % 4
+    by_place = (index // 16) * 8 + ((index // 4) % 4) * 128 + index % 4
+    for order, first in enumerate((by_band, by_place)):
+        r.p_own[order] = hot(first + core * 4 == named)
+        r.p_oth[order] = hot(first + (1 - core) * 4 == named)
+
     far_rows(1)
 
     def edges_1(i, carry):
@@ -455,7 +490,7 @@
         given = r.ab[pl.ds(at, chunk), :]
         for k in range(DEGREE):
             rows = pl.ds(k * NODES + at, chunk)
-            inner = r.base[rows, :]
+            inner = r.base[1, rows, :]
             s = sigmoid(inner)
             value = inner * s
             total = total + value
@@ -489,7 +524,6 @@
         r.lat[...] += mmt(r.rb[...], wr[layer])
 
     def return_end(slot, layer):
-        far_wait(slot)
         unpack(r.fars[slot].target)
         sender_b = (r.sback[...] + mm(r.list_t[...], r.far[...])).astype(BF)
         r.lat[...] += mmt(sender_b, ws[layer])
@@ -504,11 +538,20 @@
     halo_mesh = r.mesh_ext.at[pl.ds(NODES, 4 * HALO)]
     near_start(2, r.ns2, halo_mesh)
     return_local(1)
-    gradient(gd, 0, 256, turned(mesh_last), r.dback[...])
-    gradient(ga, 0, 512, turned(r.ob[...]), r.agg[1])
-    gradient(ga, 512, 512, turned(r.rb[...]), r.mesh[1])
-    core_start(ga)
-    near_wait(2, r.ns2, halo_mesh)
+    gradient(g_u1, 0, r.ob[...], r.agg[1])
+    core_start(g_u1)
+    gradient(g_r1, 0, r.rb[...], r.mesh[1])
+    core_start(g_r1)
+    gradient(g_de, 0, mesh_last, r.dback[...])
+    for part in range(5):
+        where_t = iota((256, NODES), 0) + part * 256
+        total_t = jnp.zeros((256, NODES), F32)
+        for k in range(DEGREE):
+            total_t = total_t + jnp.where(es[k : k + 1, :] == where_t, 1.0, 0.0)
+        r.enc_t[part * 256 : (part + 1) * 256, :] = total_t.astype(BF)
+    far_wait(2)
+    first_start(g_u1)
+    first_start(g_r1)
     sender_b1 = return_end(2, 1)
 
     out_back = r.lat[...].astype(BF)
@@ -516,42 +559,42 @@
     r.ab[...] = mmt(out_back, wu[0])
     lax.fori_loop(0, NODES // chunk, edges_back, 0)
     return_start(3)
-    core_wait(ga)
-    band_start(ga)
     return_local(0)
-    gradient(gb, 0, 512, turned(sender_b1), r.mesh[1])
-    gradient(gb, 512, 512, turned(r.ob[...]), r.agg[0])
-    gradient(gb, 1024, 512, turned(r.rb[...]), r.mesh[0])
-    core_start(gb)
+    gradient(g_su, 0, sender_b1, r.mesh[1])
+    gradient(g_su, 512, r.ob[...], r.agg[0])
+    core_start(g_su)
+    gradient(g_r0, 0, r.rb[...], r.mesh[0])
+    core_start(g_r0)
+    near_wait(2, r.ns2, halo_mesh)
     decoded = mmt(r.dwp[...], r.mesh_ext[...]).astype(BF)
     forecast = r.xp[...].astype(F32) + mm(decoded, r.dec_t[...])
     out_pred[...] = forecast[0:CHANNELS, :].astype(BF)
-    band_wait(ga)
-    plane_start(ga)
+    second_start(g_u1)
+    second_start(g_r1)
+    far_wait(3)
+    first_start(g_su)
+    first_start(g_r0)
     sender_b0 = return_end(3, 0)
 
     encode_back = (r.lat[...] * r.enc_slope[...]).astype(BF)
     input_back = mmt(encode_back, wn[...]).astype(BF)
     r.ns3[...] = mm(r.enc_t[GRID:, :], input_back).astype(BF)
     near_start(3, r.ns3, r.nr3)
-    core_wait(gb)
-    band_start(gb)
+    gradient(g_s0, 0, sender_b0, r.mesh[0])
+    core_start(g_s0)
+    gradient(g_en, 0, encode_back, r.enc_in[...])
+    core_start(g_en)
     r.gback[...] = mm(r.enc_t[0:GRID, :], input_back)
-    gradient(gc, 0, 512, turned(sender_b0), r.mesh[0])
-    gradient(gc, 512, 512, turned(encode_back), r.enc_in[...])
-    core_start(gc)
     encode_spread = hot(encode_row == iota((GRID, 4 * HALO), 0))
     near_wait(3, r.ns3, r.nr3)
+    first_start(g_s0)
+    first_start(g_en)
     r.gback[...] += mm(encode_spread, r.nr3[...])
     r.eb[...] = (r.gback[...] * r.gslope[...].astype(F32)).astype(BF)
-    gradient(gd, 256, 256, turned(r.eb[...]), r.xp[...], mmt)
-    core_start(gd)
-    core_wait(gc)
-    band_start(gc)
-    core_wait(gd)
-    band_start(gd)
-
-    total = plane_wait(ga)
+    across = mm(r.xp[...], r.eb[...]).astype(BF)
+    g_de.own[:, 256:512] = mmt(r.p_own[0], across)
+    g_de.sc[:, 256:512] = mmt(r.p_oth[0], across).astype(BF)
+    core_start(g_de)
 
     def into(ref, layer=None):
         def write(j, value):
@@ -562,25 +605,29 @@
 
         return write
 
-    deliver(total, 0, into(out_refresh, 1))
-    deliver(total, 512, into(out_target, 1))
-    band_wait(gb)
-    plane_start(gb)
-    band_wait(gc)
-    plane_start(gc)
-    band_wait(gd)
-    plane_start(gd)
-    total = plane_wait(gb)
+    second_start(g_su)
+    second_start(g_r0)
+    first_start(g_de)
+    second_start(g_s0)
+    second_start(g_en)
+    deliver(finish(g_u1), 0, into(out_refresh, 1))
+    deliver(finish(g_r1), 0, into(out_target, 1))
+    second_start(g_de)
+    total = finish(g_su)
     deliver(total, 0, into(out_source, 1))
     deliver(total, 512, into(out_refresh, 0))
-    deliver(total, 1024, into(out_target, 0))
-    total = plane_wait(gc)
-    deliver(total, 0, into(out_source, 0))
-    deliver(total, 512, into(out_encode))
-    total = plane_wait(gd)
+    deliver(finish(g_r0), 0, into(out_target, 0))
+    deliver(finish(g_s0), 0, into(out_source, 0))
+    deliver(finish(g_en), 0, into(out_encode))
+    total = finish(g_de)
     for ref, row in ((out_decode, 0), (out_embed, 8)):
         ref[:, 0:128] = total[row : row + 4, :]
         ref[:, 128:CHANNELS] = total[row + 4 : row + 8, 0 : CHANNELS - 128]
+
+
+def hand_over(*refs):
+    for source, target in zip(refs[:7], refs[7:]):
+        target[...] = source[...]
 
 
 def on_device(
@@ -602,17 +649,18 @@
     spec, tree = jax.tree.flatten(scratch())
     whole = pl.BlockSpec(memory_space=pltpu.VMEM)
     shape = jax.ShapeDtypeStruct
+    shapes = (
+        shape((CHANNELS, GRID), BF),
+        shape((4, CHANNELS), F32),
+        shape((4, LATENT), F32),
+        shape((2, 4, LATENT), F32),
+        shape((2, 4, LATENT), F32),
+        shape((2, 4, LATENT), F32),
+        shape((4, CHANNELS), F32),
+    )
     outs = pl.pallas_call(
         functools.partial(kernel, tree),
-        out_shape=(
-            shape((CHANNELS, GRID), BF),
-            shape((4, CHANNELS), F32),
-            shape((4, LATENT), F32),
-            shape((2, 4, LATENT), F32),
-            shape((2, 4, LATENT), F32),
-            shape((2, 4, LATENT), F32),
-            shape((4, CHANNELS), F32),
-        ),
+        out_shape=shapes,
         in_specs=[whole] * 14,
         out_specs=(whole,) * 7,
         scratch_shapes=spec,
@@ -635,6 +683,12 @@
         decode_lists,
         decoder_edge_sources.T,
     )
+    outs = pl.pallas_call(
+        hand_over,
+        out_shape=shapes,
+        in_specs=[whole] * 7,
+        out_specs=(whole,) * 7,
+    )(*outs)
     return (
         outs[0].T,
         outs[1].T,

time: 113 us -> 100 us (0.88)
  Pallas kernels: 106 us -> 99.5 us
  local copies, waits for them, and re-layouts: 5.76 us -> 0 us
    pallas_call x1 -> x2, Pallas kernels: 106 us -> 99.5 us  [the longest x1 97.6 us: on_device(): pl.pallas_call(functools.partial(kernel, tree), out_shape=shapes, in_spec...]
    unnamed x19 -> x0, local copies, waits for them, and re-layouts: 5.76 us -> none
where the time goes in v2:
time: 100 us
  Pallas kernels  99.5 us (100%)
    pallas_call x1, Pallas kernels, on_device(): pl.pallas_call(functools.partial(kernel, tree), out_shape=shapes, in_spec...  97.6 us

profile of v2, /device:TPU:0, one launch (start us, length us, event | category | flops | bytes accessed | tf_op | source)
XLA Modules:
  0.0 100.1 jit_solution(3625148178048279946)
XLA Ops:
  0.6 97.6 %shard_map.189 = (bf16[227,1024]{1,0:T(8,128)(2,1)}, f32[4,227]{1,0:T(4,128)}, f32[4,512]{1,0:T(4,128)}, f32[2,4,512]{2,1,0:T(4,128)}, f32[2,4,512]{2,1,0:T(4,12...) custom-call(bf16[227,1024]{1,0:T(8,128)(2,1)} %bitcast.13, bf16[227,1024]{1,0:T(8,128)(2,1)} %bitcast.14, ...), custom_call_target="tpu_custom_call" | custom-call | tf_op jit(solution)/shard_map/pallas_call | solution.py:661
  98.3 1.9 %shard_map.190 = (bf16[227,1024]{1,0:T(8,128)(2,1)}, f32[4,227]{1,0:T(4,128)}, f32[4,512]{1,0:T(4,128)}, f32[2,4,512]{2,1,0:T(4,128)}, f32[2,4,512]{2,1,0:T(4,12...) custom-call(bf16[227,1024]{1,0:T(8,128)(2,1)} %get-tuple-element.21.refs_0_, f32[4,227]{1,0:T(4,128)} %get-tuple-element.22.refs_1_, ...), custom_call_target="tpu_custom_call" | custom-call | tf_op jit(solution)/shard_map/pallas_call | solution.py:686

commit v3 on v2

--- a/solution.py
+++ b/solution.py
@@ -86,6 +86,8 @@
         slope=vm((EDGES, LATENT), BF),
         ib=vm((EDGES, LATENT), BF),
         rb=vm((NODES, LATENT), BF),
+        back=vm((NODES, LATENT), F32),
+        total=vm((NODES, LATENT), F32),
         ab=vm((NODES, LATENT), F32),
         ob=vm((NODES, LATENT), BF),
         lat=vm((NODES, LATENT), F32),
@@ -105,6 +107,13 @@
         nr3=vm((4 * HALO, LATENT), BF),
         near_sem=sems((4, 2)),
         far_sem=sems((4, 2)),
+        entered=pltpu.SemaphoreType.REGULAR,
+        cot=vm((CHANNELS, GRID), BF),
+        wn=vm((LATENT, LATENT), BF),
+        ws=vm((2, LATENT, LATENT), BF),
+        wr=vm((2, LATENT, LATENT), BF),
+        wu=vm((2, LATENT, LATENT), BF),
+        load_sem=sems((5,)),
         fars=[dict(source=vm((4 * FAR, 128), BF), target=vm((4 * FAR, 128), BF)) for _ in range(4)],
         groups=[
             dict(
@@ -123,7 +132,7 @@
     )
 
 
-def kernel(tree, xt, ct, we, wn, ws, wr, wu, dwt, el, es, ml, ms, dl, ds_, *rest):
+def kernel(tree, xt, ct_far, we, wn_far, ws_far, wr_far, wu_far, dwt, el, es, ml, ms, dl, ds_, *rest):
     out_pred, out_embed, out_encode, out_source, out_target, out_refresh, out_decode = rest[:7]
     r = Refs(jax.tree.unflatten(tree, rest[7:]))
     for each, (width, along) in zip(r.groups, GROUPS):
@@ -138,12 +147,18 @@
     barrier = pltpu.get_barrier_semaphore()
 
     def greet(t, carry):
-        u = lax.rem(b + t // SECTORS, BANDS)
-        v = lax.rem(c + lax.rem(t, SECTORS), SECTORS)
-        pl.semaphore_signal(barrier, inc=1, device_id=(u, v), device_id_type=MESH)
+        v = lax.rem(c + t, SECTORS)
+        pl.semaphore_signal(barrier, inc=1, device_id=(b, v), device_id_type=MESH)
         return carry
 
-    lax.fori_loop(1, PEERS, greet, 0)
+    lax.fori_loop(1, SECTORS, greet, 0)
+
+    def greet_bands(semaphore):
+        for t in range(1, BANDS):
+            u = lax.rem(b + t, BANDS)
+            pl.semaphore_signal(semaphore, inc=1, device_id=(u, c), device_id_type=MESH)
+
+    greet_bands(barrier)
 
     neighbours = (
         (b, lax.rem(c + SECTORS - 1, SECTORS)),
@@ -197,6 +212,7 @@
         drain(r.fars[i].source.at[rest_of], r.far_sem.at[i, 0])
 
     packed = r.packed
+    chunk = 32
 
     def pack(value, target):
         for i in range(SLOTS):
@@ -331,7 +347,17 @@
             row = 4 * (at // 128 + j)
             write(j, total[row : row + 4, :])
 
-    for target, source in ((r.xp, xt), (r.cp, ct), (r.wep, we), (r.dwp, dwt)):
+    wn, ws, wr, wu = r.wn, r.ws, r.wr, r.wu
+    loads = [
+        pltpu.make_async_copy(source, target, r.load_sem.at[i])
+        for i, (source, target) in enumerate(
+            ((wn_far, wn), (ws_far, ws), (wr_far, wr), (wu_far, wu), (ct_far, r.cot))
+        )
+    ]
+    for each in loads:
+        each.start()
+
+    for target, source in ((r.xp, xt), (r.wep, we), (r.dwp, dwt)):
         target[224:256, :] = jnp.zeros((32, source.shape[1]), BF)
         target[0:CHANNELS, :] = source[...]
 
@@ -354,9 +380,14 @@
     encode_pick = hot(column(encode_row) == iota((4 * HALO, GRID), 1))
     r.ns0[...] = mm(encode_pick, r.grid_ext[0:GRID, :]).astype(BF)
 
-    pl.semaphore_wait(barrier, PEERS - 1)
+    pl.semaphore_wait(barrier, SECTORS - 1 + BANDS - 1)
+    greet_bands(r.entered)
     halo_grid = r.grid_ext.at[pl.ds(GRID, 4 * HALO)]
     near_start(0, r.ns0, halo_grid)
+    for each in loads:
+        each.wait()
+    r.cp[224:256, :] = jnp.zeros((32, GRID), BF)
+    r.cp[0:CHANNELS, :] = r.cot[...]
 
     es_col = jnp.transpose(es[...])
     for part in range(5):
@@ -392,17 +423,29 @@
             rows = slice(k * NODES, (k + 1) * NODES)
             r.base[layer, rows, :] = mm(r.oh_loc[rows, :], sender) + receiver
 
-    def far_rows(layer):
+    def far_rows(layer, edge):
         far_wait(layer)
         unpack(r.fars[layer].target)
+        r.total[...] = jnp.zeros((NODES, LATENT), F32)
 
         def add(k, carry):
-            rows = pl.ds(pl.multiple_of(k * NODES, NODES), NODES)
-            r.base[layer, rows, :] += mm(r.oh_far[rows, :], r.far[...])
+            at = pl.multiple_of(k * NODES, NODES)
+            rows = pl.ds(at, NODES)
+            far = mm(r.oh_far[rows, :], r.far[...])
+            for h in range(NODES // chunk):
+                part = slice(h * chunk, (h + 1) * chunk)
+                rows = pl.ds(at + h * chunk, chunk)
+                inner = r.base[layer, rows, :] + far[part, :]
+                s = sigmoid(inner)
+                value = inner * s
+                r.total[part, :] += value
+                edge(inner, s, value, part, rows)
             return carry
 
         lax.fori_loop(0, DEGREE, add, 0)
-
+        r.agg[layer] = r.total[...].astype(BF)
+
+    pl.semaphore_wait(r.entered, BANDS - 1)
     sender = send_rows(0)
 
     def far_index(v):
@@ -429,19 +472,10 @@
     near_start(1, r.ns1, r.nr1)
     r.dext[...] = mmt(r.dec_t[0:NODES, :], r.cp[...])
 
-    far_rows(0)
-    chunk = 32
-
-    def edges_0(i, carry):
-        at = pl.multiple_of(i * chunk, chunk)
-        total = jnp.zeros((chunk, LATENT), F32)
-        for k in range(DEGREE):
-            inner = r.base[0, pl.ds(k * NODES + at, chunk), :]
-            total = total + inner * sigmoid(inner)
-        r.agg[0, pl.ds(at, chunk), :] = total.astype(BF)
-        return carry
-
-    lax.fori_loop(0, NODES // chunk, edges_0, 0)
+    def keep(inner, s, value, part, rows):
+        r.base[0, rows, :] = inner
+
+    far_rows(0, keep)
     r.mesh[1] = (r.mesh[0].astype(F32) + mm(r.agg[0], wu[0])).astype(BF)
 
     sender = send_rows(1)
@@ -481,27 +515,15 @@
         r.p_own[order] = hot(first + core * 4 == named)
         r.p_oth[order] = hot(first + (1 - core) * 4 == named)
 
-    far_rows(1)
-
-    def edges_1(i, carry):
-        at = pl.multiple_of(i * chunk, chunk)
-        total = jnp.zeros((chunk, LATENT), F32)
-        back = jnp.zeros((chunk, LATENT), F32)
-        given = r.ab[pl.ds(at, chunk), :]
-        for k in range(DEGREE):
-            rows = pl.ds(k * NODES + at, chunk)
-            inner = r.base[1, rows, :]
-            s = sigmoid(inner)
-            value = inner * s
-            total = total + value
-            edge = given * (s + value * (1.0 - s))
-            back = back + edge
-            r.ib[rows, :] = edge.astype(BF)
-        r.agg[1, pl.ds(at, chunk), :] = total.astype(BF)
-        r.rb[pl.ds(at, chunk), :] = back.astype(BF)
-        return carry
-
-    lax.fori_loop(0, NODES // chunk, edges_1, 0)
+    r.back[...] = jnp.zeros((NODES, LATENT), F32)
+
+    def turn(inner, s, value, part, rows):
+        back = r.ab[part, :] * (s + value * (1.0 - s))
+        r.back[part, :] += back
+        r.ib[rows, :] = back.astype(BF)
+
+    far_rows(1, turn)
+    r.rb[...] = r.back[...].astype(BF)
 
     def edges_back(i, carry):
         at = pl.multiple_of(i * chunk, chunk)
@@ -549,9 +571,9 @@
         for k in range(DEGREE):
             total_t = total_t + jnp.where(es[k : k + 1, :] == where_t, 1.0, 0.0)
         r.enc_t[part * 256 : (part + 1) * 256, :] = total_t.astype(BF)
-    far_wait(2)
     first_start(g_u1)
     first_start(g_r1)
+    far_wait(2)
     sender_b1 = return_end(2, 1)
 
     out_back = r.lat[...].astype(BF)
@@ -569,11 +591,11 @@
     decoded = mmt(r.dwp[...], r.mesh_ext[...]).astype(BF)
     forecast = r.xp[...].astype(F32) + mm(decoded, r.dec_t[...])
     out_pred[...] = forecast[0:CHANNELS, :].astype(BF)
+    first_start(g_su)
+    first_start(g_r0)
     second_start(g_u1)
     second_start(g_r1)
     far_wait(3)
-    first_start(g_su)
-    first_start(g_r0)
     sender_b0 = return_end(3, 0)
 
     encode_back = (r.lat[...] * r.enc_slope[...]).astype(BF)
@@ -586,9 +608,11 @@
     core_start(g_en)
     r.gback[...] = mm(r.enc_t[0:GRID, :], input_back)
     encode_spread = hot(encode_row == iota((GRID, 4 * HALO), 0))
-    near_wait(3, r.ns3, r.nr3)
     first_start(g_s0)
     first_start(g_en)
+    second_start(g_su)
+    second_start(g_r0)
+    near_wait(3, r.ns3, r.nr3)
     r.gback[...] += mm(encode_spread, r.nr3[...])
     r.eb[...] = (r.gback[...] * r.gslope[...].astype(F32)).astype(BF)
     across = mm(r.xp[...], r.eb[...]).astype(BF)
@@ -605,8 +629,6 @@
 
         return write
 
-    second_start(g_su)
-    second_start(g_r0)
     first_start(g_de)
     second_start(g_s0)
     second_start(g_en)
@@ -648,6 +670,7 @@
 ):
     spec, tree = jax.tree.flatten(scratch())
     whole = pl.BlockSpec(memory_space=pltpu.VMEM)
+    far = pl.BlockSpec(memory_space=pl.ANY)
     shape = jax.ShapeDtypeStruct
     shapes = (
         shape((CHANNELS, GRID), BF),
@@ -661,7 +684,7 @@
     outs = pl.pallas_call(
         functools.partial(kernel, tree),
         out_shape=shapes,
-        in_specs=[whole] * 14,
+        in_specs=[whole, far, whole, far, far, far, far] + [whole] * 7,
         out_specs=(whole,) * 7,
         scratch_shapes=spec,
         compiler_params=pltpu.CompilerParams(

time: 100 us -> 91.6 us (0.916)
  Pallas kernels: 99.5 us -> 90.7 us
    pallas_call x1, Pallas kernels: 97.6 us -> 88.8 us  [on_device(): pl.pallas_call(functools.partial(kernel, tree), out_shape=shapes, in_spec...]
where the time goes in v3:
time: 91.6 us; the launch traced here: 91.3 us
  Pallas kernels  90.7 us (99%)
    pallas_call x1, Pallas kernels, on_device(): pl.pallas_call(functools.partial(kernel, tree), out_shape=shapes, in_spec...  88.8 us
    pallas_call x1, Pallas kernels, on_device(): pl.pallas_call(hand_over, out_shape=shapes, in_specs=[whole] * 7, out_spe...  1.89 us

profile of v3, /device:TPU:0, one launch (start us, length us, event | category | flops | bytes accessed | tf_op | source)
XLA Modules:
  0.0 91.3 jit_solution(15224025038617852390)
XLA Ops:
  0.6 88.8 %shard_map.189 = (bf16[227,1024]{1,0:T(8,128)(2,1)}, f32[4,227]{1,0:T(4,128)}, f32[4,512]{1,0:T(4,128)}, f32[2,4,512]{2,1,0:T(4,128)}, f32[2,4,512]{2,1,0:T(4,12...) custom-call(bf16[227,1024]{1,0:T(8,128)(2,1)} %bitcast.13, bf16[227,1024]{1,0:T(8,128)(2,1)} %bitcast.14, ...), custom_call_target="tpu_custom_call" | custom-call | tf_op jit(solution)/shard_map/pallas_call | solution.py:684
  89.5 1.9 %shard_map.190 = (bf16[227,1024]{1,0:T(8,128)(2,1)}, f32[4,227]{1,0:T(4,128)}, f32[4,512]{1,0:T(4,128)}, f32[2,4,512]{2,1,0:T(4,128)}, f32[2,4,512]{2,1,0:T(4,12...) custom-call(bf16[227,1024]{1,0:T(8,128)(2,1)} %get-tuple-element.21.refs_0_, f32[4,227]{1,0:T(4,128)} %get-tuple-element.22.refs_1_, ...), custom_call_target="tpu_custom_call" | custom-call | tf_op jit(solution)/shard_map/pallas_call | solution.py:709

commit v4 on v3

--- a/solution.py
+++ b/solution.py
@@ -106,7 +106,7 @@
         ns3=vm((4 * HALO, LATENT), BF),
         nr3=vm((4 * HALO, LATENT), BF),
         near_sem=sems((4, 2)),
-        far_sem=sems((4, 2)),
+        far_sem=sems((4, 2, 2)),
         entered=pltpu.SemaphoreType.REGULAR,
         cot=vm((CHANNELS, GRID), BF),
         wn=vm((LATENT, LATENT), BF),
@@ -185,49 +185,70 @@
         drain(target, r.near_sem.at[i, 1])
         drain(source, r.near_sem.at[i, 0])
 
-    def far_start(i):
+    half = PEERS // 2
+    deep, wide = c // 8, lax.rem(c // 2, 4)
+
+    def peer(t, sign):
+        w = half - 1 - lax.rem(t, half)
+        u = lax.rem(b + BANDS + sign * lax.rem(w, 4), BANDS)
+        z = lax.rem(deep + 4 + sign * lax.rem(w // 4, 4), 4)
+        y = lax.rem(wide + 4 + sign * (w // 16), 4)
+        return u, z * 8 + y * 2 + lax.rem(core + t // half, 2)
+
+    def block(at):
+        return pl.ds(pl.multiple_of(at * 16, 16), 16)
+
+    def far_start(i, group, back):
         source, target = r.fars[i].source, r.fars[i].target
-        mine = pl.ds(pl.multiple_of(me * 16, 16), 16)
 
         def send(t, carry):
-            u = lax.rem(b + lax.rem(t, BANDS), BANDS)
-            v = lax.rem(c + t // BANDS, SECTORS)
-            block = pl.ds(pl.multiple_of((u * SECTORS + v) * 16, 16), 16)
+            u, v = peer(t, -1 if back else 1)
+            there = u * SECTORS + v
             pltpu.make_async_remote_copy(
-                source.at[block],
-                target.at[mine],
-                r.far_sem.at[i, 0],
-                r.far_sem.at[i, 1],
+                source.at[block(t if back else there)],
+                target.at[block(me if back else t)],
+                r.far_sem.at[i, group, 0],
+                r.far_sem.at[i, group, 1],
                 device_id=(u, v),
                 device_id_type=MESH,
             ).start()
             return carry
 
-        lax.fori_loop(1, PEERS, send, 0)
-        target[mine, :] = source[mine, :]
-
-    def far_wait(i):
-        rest_of = pl.ds(0, 16 * (PEERS - 1))
-        drain(r.fars[i].target.at[rest_of], r.far_sem.at[i, 1])
-        drain(r.fars[i].source.at[rest_of], r.far_sem.at[i, 0])
+        if group == 0:
+            lax.fori_loop(0, half - 1, send, 0)
+            if back:
+                target[block(me), :] = source[16 * (half - 1) : 16 * half, :]
+            else:
+                target[16 * (half - 1) : 16 * half, :] = source[block(me), :]
+        else:
+            lax.fori_loop(half, PEERS, send, 0)
+
+    def far_wait(i, group):
+        part = pl.ds(0, 16 * (half - 1 + group))
+        drain(r.fars[i].target.at[part], r.far_sem.at[i, group, 1])
+        drain(r.fars[i].source.at[part], r.far_sem.at[i, group, 0])
 
     packed = r.packed
     chunk = 32
 
-    def pack(value, target):
+    def pack(value, target, first=0):
+        peers = value.shape[0] // SLOTS
         for i in range(SLOTS):
             for j in range(4):
-                packed[pl.ds(4 * j + i, PEERS, stride=16), :] = value[
-                    i * PEERS : (i + 1) * PEERS, j * 128 : (j + 1) * 128
+                packed[pl.ds(first * 16 + 4 * j + i, peers, stride=16), :] = value[
+                    i * peers : (i + 1) * peers, j * 128 : (j + 1) * 128
                 ]
-        target[...] = packed[...].astype(BF)
-
-    def unpack(source):
-        packed[...] = source[...].astype(F32)
+        rows = slice(first * 16, (first + peers) * 16)
+        target[rows, :] = packed[rows, :].astype(BF)
+
+    def unpack(source, first=0, peers=PEERS):
+        rows = slice(first * 16, (first + peers) * 16)
+        packed[rows, :] = source[rows, :].astype(F32)
         for i in range(SLOTS):
+            at = first * SLOTS + i * peers
             for j in range(4):
-                r.far[i * PEERS : (i + 1) * PEERS, j * 128 : (j + 1) * 128] = packed[
-                    pl.ds(4 * j + i, PEERS, stride=16), :
+                r.far[at : at + peers, j * 128 : (j + 1) * 128] = packed[
+                    pl.ds(first * 16 + 4 * j + i, peers, stride=16), :
                 ].astype(BF)
 
     def turned(g, value):
@@ -414,7 +435,8 @@
     def send_rows(layer):
         sender = mm(r.mesh[layer], ws[layer]).astype(BF)
         pack(mm(r.list_r[...], sender), r.fars[layer].source)
-        far_start(layer)
+        far_start(layer, 0, False)
+        far_start(layer, 1, False)
         return sender
 
     def local_rows(layer, sender):
@@ -424,14 +446,23 @@
             r.base[layer, rows, :] = mm(r.oh_loc[rows, :], sender) + receiver
 
     def far_rows(layer, edge):
-        far_wait(layer)
-        unpack(r.fars[layer].target)
+        far_wait(layer, 0)
+        unpack(r.fars[layer].target, 0, half)
+
+        def first(k, carry):
+            rows = pl.ds(pl.multiple_of(k * NODES, NODES), NODES)
+            r.base[layer, rows, :] += mm(r.oh_far[rows, 0 : FAR // 2], r.far[0 : FAR // 2, :])
+            return carry
+
+        lax.fori_loop(0, DEGREE, first, 0)
+        far_wait(layer, 1)
+        unpack(r.fars[layer].target, half, half)
         r.total[...] = jnp.zeros((NODES, LATENT), F32)
 
         def add(k, carry):
             at = pl.multiple_of(k * NODES, NODES)
             rows = pl.ds(at, NODES)
-            far = mm(r.oh_far[rows, :], r.far[...])
+            far = mm(r.oh_far[rows, FAR // 2 :], r.far[FAR // 2 :, :])
             for h in range(NODES // chunk):
                 part = slice(h * chunk, (h + 1) * chunk)
                 rows = pl.ds(at + h * chunk, chunk)
@@ -450,7 +481,10 @@
 
     def far_index(v):
         k = v - NODES
-        return jnp.where(k >= 0, (k & 3) * PEERS + (k >> 2), -1)
+        p = k >> 2
+        w = ((b - (p >> 5)) & 3) + 4 * ((deep - (p >> 3)) & 3) + 16 * ((wide - (p >> 1)) & 3)
+        group = (core - p) & 1
+        return jnp.where(k >= 0, group * (FAR // 2) + (k & 3) * half + half - 1 - w, -1)
 
     ms_row = ms[...]
     ms_col = jnp.transpose(ms_row)
@@ -538,8 +572,10 @@
         return carry
 
     def return_start(slot):
-        pack(mm(r.t_far[...], r.ib[...]), r.fars[slot].source)
-        far_start(slot)
+        for group in range(2):
+            rows = slice(group * (FAR // 2), (group + 1) * (FAR // 2))
+            pack(mm(r.t_far[rows, :], r.ib[...]), r.fars[slot].source, group * half)
+            far_start(slot, group, True)
 
     def return_local(layer):
         r.sback[...] = mm(r.t_loc[...], r.ib[...])
@@ -573,7 +609,8 @@
         r.enc_t[part * 256 : (part + 1) * 256, :] = total_t.astype(BF)
     first_start(g_u1)
     first_start(g_r1)
-    far_wait(2)
+    far_wait(2, 0)
+    far_wait(2, 1)
     sender_b1 = return_end(2, 1)
 
     out_back = r.lat[...].astype(BF)
@@ -595,7 +632,8 @@
     first_start(g_r0)
     second_start(g_u1)
     second_start(g_r1)
-    far_wait(3)
+    far_wait(3, 0)
+    far_wait(3, 1)
     sender_b0 = return_end(3, 0)
 
     encode_back = (r.lat[...] * r.enc_slope[...]).astype(BF)

time: 91.6 us -> 89.9 us (0.981)
  Pallas kernels: 90.7 us -> 89.1 us
    pallas_call x1, Pallas kernels: 88.8 us -> 87.2 us  [on_device(): pl.pallas_call(functools.partial(kernel, tree), out_shape=shapes, in_spec...]
where the time goes in v4:
time: 89.9 us; the launch traced here: 89.8 us
  Pallas kernels  89.1 us (99%)
    pallas_call x1, Pallas kernels, on_device(): pl.pallas_call(functools.partial(kernel, tree), out_shape=shapes, in_spec...  87.2 us
    pallas_call x1, Pallas kernels, on_device(): pl.pallas_call(hand_over, out_shape=shapes, in_specs=[whole] * 7, out_spe...  1.89 us

profile of v4, /device:TPU:0, one launch (start us, length us, event | category | flops | bytes accessed | tf_op | source)
XLA Modules:
  0.0 89.8 jit_solution(2609889246660542940)
XLA Ops:
  0.6 87.2 %shard_map.189 = (bf16[227,1024]{1,0:T(8,128)(2,1)}, f32[4,227]{1,0:T(4,128)}, f32[4,512]{1,0:T(4,128)}, f32[2,4,512]{2,1,0:T(4,128)}, f32[2,4,512]{2,1,0:T(4,12...) custom-call(bf16[227,1024]{1,0:T(8,128)(2,1)} %bitcast.13, bf16[227,1024]{1,0:T(8,128)(2,1)} %bitcast.14, ...), custom_call_target="tpu_custom_call" | custom-call | tf_op jit(solution)/shard_map/pallas_call | solution.py:722
  87.9 1.9 %shard_map.190 = (bf16[227,1024]{1,0:T(8,128)(2,1)}, f32[4,227]{1,0:T(4,128)}, f32[4,512]{1,0:T(4,128)}, f32[2,4,512]{2,1,0:T(4,128)}, f32[2,4,512]{2,1,0:T(4,12...) custom-call(bf16[227,1024]{1,0:T(8,128)(2,1)} %get-tuple-element.21.refs_0_, f32[4,227]{1,0:T(4,128)} %get-tuple-element.22.refs_1_, ...), custom_call_target="tpu_custom_call" | custom-call | tf_op jit(solution)/shard_map/pallas_call | solution.py:747

commit v5 on v4

--- a/solution.py
+++ b/solution.py
@@ -54,7 +54,15 @@
             setattr(self, name, ref)
 
 
-GROUPS = ((512, True), (512, False), (1024, True), (512, False), (512, True), (512, False), (512, True))
+GROUPS = (
+    (512, True),
+    (512, False),
+    (256, True),
+    (1024, True),
+    (512, False),
+    (1024, False),
+    (256, True),
+)
 
 
 def scratch():
@@ -123,8 +131,8 @@
                 sx=vm((NODES, width), BF),
                 rx=vm((192 if along else NODES, width), BF),
                 fp=vm((width // 2 if along else width // 8, 128), F32),
-                sp=vm((width // 2 if along else width // 8, 128), BF),
-                rp=vm((width // 2 if along else 3 * width // 32, 128), BF),
+                sp=vm((width // 2 if along else width // 8, 128), BF if width > 256 else F32),
+                rp=vm((width // 2 if along else 3 * width // 32, 128), BF if width > 256 else F32),
                 sem=sems((3, 2)),
             )
             for width, along in GROUPS
@@ -137,7 +145,7 @@
     r = Refs(jax.tree.unflatten(tree, rest[7:]))
     for each, (width, along) in zip(r.groups, GROUPS):
         each.along = along
-    g_u1, g_r1, g_su, g_r0, g_s0, g_en, g_de = r.groups
+    g_u1, g_r1, g_dc, g_su, g_r0, g_se, g_em = r.groups
     b = lax.axis_index("lat")
     c = lax.axis_index("lon")
     me = b * SECTORS + c
@@ -294,12 +302,12 @@
             ).start()
 
     def over_plane(g, hop, source, target, rows):
-        mine = pl.ds(pl.multiple_of(place * rows, 16), rows)
+        mine = pl.ds(pl.multiple_of(place * rows, min(rows, 16)), rows)
 
         def send(t, carry):
             q = lax.rem(place + t, 16)
             pltpu.make_async_remote_copy(
-                source.at[pl.ds(pl.multiple_of(q * rows, 16), rows)],
+                source.at[pl.ds(pl.multiple_of(q * rows, min(rows, 16)), rows)],
                 target.at[mine],
                 g.sem.at[hop, 0],
                 g.sem.at[hop, 1],
@@ -351,7 +359,7 @@
                 for j in range(width // 128):
                     at = u * rows + 4 * j
                     g.fp[at : at + 4, :] = total[u * 4 : (u + 1) * 4, j * 128 : (j + 1) * 128]
-        g.sp[...] = g.fp[...].astype(BF)
+        g.sp[...] = g.fp[...].astype(g.sp.dtype)
         if g.along:
             over_plane(g, 2, g.sp, g.rp, rows)
         else:
@@ -600,7 +608,8 @@
     core_start(g_u1)
     gradient(g_r1, 0, r.rb[...], r.mesh[1])
     core_start(g_r1)
-    gradient(g_de, 0, mesh_last, r.dback[...])
+    gradient(g_dc, 0, mesh_last, r.dback[...])
+    core_start(g_dc)
     for part in range(5):
         where_t = iota((256, NODES), 0) + part * 256
         total_t = jnp.zeros((256, NODES), F32)
@@ -609,6 +618,7 @@
         r.enc_t[part * 256 : (part + 1) * 256, :] = total_t.astype(BF)
     first_start(g_u1)
     first_start(g_r1)
+    first_start(g_dc)
     far_wait(2, 0)
     far_wait(2, 1)
     sender_b1 = return_end(2, 1)
@@ -632,6 +642,7 @@
     first_start(g_r0)
     second_start(g_u1)
     second_start(g_r1)
+    second_start(g_dc)
     far_wait(3, 0)
     far_wait(3, 1)
     sender_b0 = return_end(3, 0)
@@ -640,23 +651,21 @@
     input_back = mmt(encode_back, wn[...]).astype(BF)
     r.ns3[...] = mm(r.enc_t[GRID:, :], input_back).astype(BF)
     near_start(3, r.ns3, r.nr3)
-    gradient(g_s0, 0, sender_b0, r.mesh[0])
-    core_start(g_s0)
-    gradient(g_en, 0, encode_back, r.enc_in[...])
-    core_start(g_en)
+    gradient(g_se, 0, sender_b0, r.mesh[0])
+    gradient(g_se, 512, encode_back, r.enc_in[...])
+    core_start(g_se)
     r.gback[...] = mm(r.enc_t[0:GRID, :], input_back)
     encode_spread = hot(encode_row == iota((GRID, 4 * HALO), 0))
-    first_start(g_s0)
-    first_start(g_en)
+    first_start(g_se)
     second_start(g_su)
     second_start(g_r0)
     near_wait(3, r.ns3, r.nr3)
     r.gback[...] += mm(encode_spread, r.nr3[...])
     r.eb[...] = (r.gback[...] * r.gslope[...].astype(F32)).astype(BF)
     across = mm(r.xp[...], r.eb[...]).astype(BF)
-    g_de.own[:, 256:512] = mmt(r.p_own[0], across)
-    g_de.sc[:, 256:512] = mmt(r.p_oth[0], across).astype(BF)
-    core_start(g_de)
+    g_em.sc[...] = mmt(r.p_oth[0], across).astype(BF)
+    core_start(g_em)
+    g_em.own[...] = mmt(r.p_own[0], across)
 
     def into(ref, layer=None):
         def write(j, value):
@@ -667,22 +676,24 @@
 
         return write
 
-    first_start(g_de)
-    second_start(g_s0)
-    second_start(g_en)
+    def deliver_padded(total, ref):
+        ref[:, 0:128] = total[0:4, :]
+        ref[:, 128:CHANNELS] = total[4:8, 0 : CHANNELS - 128]
+
     deliver(finish(g_u1), 0, into(out_refresh, 1))
     deliver(finish(g_r1), 0, into(out_target, 1))
-    second_start(g_de)
+    first_start(g_em)
+    deliver_padded(finish(g_dc), out_decode)
     total = finish(g_su)
     deliver(total, 0, into(out_source, 1))
     deliver(total, 512, into(out_refresh, 0))
     deliver(finish(g_r0), 0, into(out_target, 0))
-    deliver(finish(g_s0), 0, into(out_source, 0))
-    deliver(finish(g_en), 0, into(out_encode))
-    total = finish(g_de)
-    for ref, row in ((out_decode, 0), (out_embed, 8)):
-        ref[:, 0:128] = total[row : row + 4, :]
-        ref[:, 128:CHANNELS] = total[row + 4 : row + 8, 0 : CHANNELS - 128]
+    second_start(g_se)
+    second_start(g_em)
+    total = finish(g_se)
+    deliver(total, 0, into(out_source, 0))
+    deliver(total, 512, into(out_encode))
+    deliver_padded(finish(g_em), out_embed)
 
 
 def hand_over(*refs):

time: 89.9 us -> 89.1 us (level)
  no operation moved by 1% of the time
where the time goes in v5:
time: 89.1 us; the launch traced here: 89 us
  Pallas kernels  88.3 us (99%)
    pallas_call x1, Pallas kernels, on_device(): pl.pallas_call(functools.partial(kernel, tree), out_shape=shapes, in_spec...  86.5 us
    pallas_call x1, Pallas kernels, on_device(): pl.pallas_call(hand_over, out_shape=shapes, in_specs=[whole] * 7, out_spe...  1.89 us

profile of v5, /device:TPU:0, one launch (start us, length us, event | category | flops | bytes accessed | tf_op | source)
XLA Modules:
  0.0 89.0 jit_solution(7942439489806462276)
XLA Ops:
  0.6 86.5 %shard_map.189 = (bf16[227,1024]{1,0:T(8,128)(2,1)}, f32[4,227]{1,0:T(4,128)}, f32[4,512]{1,0:T(4,128)}, f32[2,4,512]{2,1,0:T(4,128)}, f32[2,4,512]{2,1,0:T(4,12...) custom-call(bf16[227,1024]{1,0:T(8,128)(2,1)} %bitcast.13, bf16[227,1024]{1,0:T(8,128)(2,1)} %bitcast.14, ...), custom_call_target="tpu_custom_call" | custom-call | tf_op jit(solution)/shard_map/pallas_call | solution.py:733
  87.1 1.9 %shard_map.190 = (bf16[227,1024]{1,0:T(8,128)(2,1)}, f32[4,227]{1,0:T(4,128)}, f32[4,512]{1,0:T(4,128)}, f32[2,4,512]{2,1,0:T(4,128)}, f32[2,4,512]{2,1,0:T(4,12...) custom-call(bf16[227,1024]{1,0:T(8,128)(2,1)} %get-tuple-element.21.refs_0_, f32[4,227]{1,0:T(4,128)} %get-tuple-element.22.refs_1_, ...), custom_call_target="tpu_custom_call" | custom-call | tf_op jit(solution)/shard_map/pallas_call | solution.py:758
